TPU v7x, 512 devices: a whole 4x8x8 slice. The times are simulated.
512 devices in a mesh: gx: 16 (over z, core), gy: 4 (over y_hi), gz: 8 (over y_lo, x).
Axes of the slice: x: 4, y: 8 (y_hi: 4, y_lo: 2; y = y_hi * 2 + y_lo), z: 8, core: 2. Of those that a mesh axis runs over, the one named last changes fastest.
Arguments:
- features: bfloat16 [16, 4, 8, 128, 128], P('gx', 'gy', 'gz'), may hold values from -6 to 6
- positions: float32 [16, 4, 8, 3, 128], P('gx', 'gy', 'gz'), may hold values from 0 to 11
- w_up: bfloat16 [128, 128], replicated, may hold values from -0.5 to 0.5
- w_basis: float32 [8, 64], replicated, may hold values from -2 to 2
- w_hidden: bfloat16 [64, 64], replicated, may hold values from -0.75 to 0.75
- w_radial: bfloat16 [64, 384], replicated, may hold values from -0.75 to 0.75
- w_mix: bfloat16 [384, 128], replicated, may hold values from -0.3125 to 0.3125
- w_read: float32 [128, 16], replicated, may hold values from -0.5 to 0.5
- w_out: float32 [16], replicated, may hold values from -1.5 to 1.5
- send_lists: int32 [16, 4, 8, 3, 3, 3, 64], P('gx', 'gy', 'gz'), may hold values from 0 to 127, as said below
- tile_senders: int32 [16, 4, 8, 64, 128], P('gx', 'gy', 'gz'), may hold values from 0 to 1807, as said below
- tile_slots: int32 [16, 4, 8, 64, 128], P('gx', 'gy', 'gz'), may hold values from 0 to 8, as said below
- tile_bases: int32 [16, 4, 8, 64], P('gx', 'gy', 'gz'), may hold values from 0 to 120
- tile_live: int32 [16, 4, 8], P('gx', 'gy', 'gz'), may hold values from 16 to 64, as said below
Outputs:
- forces: float32 [16, 4, 8, 3, 128], P('gx', 'gy', 'gz')
- atom_energy: float32 [16, 4, 8, 128], P('gx', 'gy', 'gz')
Inputs may be any that keep to these rules, and one draw needn't show every extreme that they name: `send_lists`: for direction (dx, dy, dz), entry [.., 1 + dx, 1 + dy, 1 + dz, s] names an atom of the device; with k nonzero components the first 64 * 2 / 2**k entries (k of 1 to 3) name distinct atoms, those lying in the half of the cube toward each nonzero component, and later entries name other atoms. The list with dx = dy = dz = 0 is never read. `tile_senders`: below 128: an atom of the device. Else 128 + b * 64 + s: entry s of the atoms arriving from direction b; b = 13 never occurs, and s < 64 * 2 / 2**k for k nonzero components of the direction. `tile_slots`: the value 8 marks an unused edge. `tile_live`: A quarter of the devices have 64 live tiles, the others between 16 and 21.
All inputs are finite; a program needn't handle non-finite values.
Results may differ from a plain program's by a relative error of at most 0.022.
Values may be sent and summed in bfloat16 or wider, within the bound.
A program may use at most 64 MiB of HBM per device.

v0:
```python
import jax
import jax.numpy as jnp
from jax import lax
from jax.sharding import PartitionSpec as P

RT = 8


inv_cutoff = 0.2
domain_side = 11.0
sums_scale = 0.5


def extended(value, sides, width):
    for axis, dim in sides:
        size, length = (lax.axis_size(axis), value.shape[dim])
        up = [(i, (i + 1) % size) for i in range(size)]
        down = [(j, i) for i, j in up]
        last = lax.slice_in_dim(value, length - width, length, axis=dim)
        leading = lax.slice_in_dim(value, 0, width, axis=dim)
        before = lax.ppermute(last, axis, up)
        after = lax.ppermute(leading, axis, down)
        value = jnp.concatenate([before, value, after], axis=dim)
    return value


def harmonics(scaled):
    xcoord = scaled[0]
    ycoord = scaled[1]
    zcoord = scaled[2]
    root_three = 3.0**0.5
    root_five = 5.0**0.5
    root_fifteen = 15.0**0.5
    pieces = [
        jnp.ones_like(xcoord),
        root_three * xcoord,
        root_three * ycoord,
        root_three * zcoord,
        root_fifteen * xcoord * ycoord,
        root_fifteen * ycoord * zcoord,
        0.5 * root_five * (2.0 * zcoord * zcoord - xcoord * xcoord - ycoord * ycoord),
        root_fifteen * xcoord * zcoord,
        0.5 * root_fifteen * (xcoord * xcoord - ycoord * ycoord),
    ]
    return jnp.stack(pieces, axis=0)


def tile_sums(separation, sender_rows, slot_ids, w_basis, w_hidden, w_radial):
    edge_count, channels = sender_rows.shape
    scaled = separation * inv_cutoff
    radius_sq = jnp.sum(scaled * scaled, axis=0)
    envelope = jnp.maximum(1.0 - radius_sq * radius_sq, 0.0) ** 2
    decays = (jnp.arange(w_basis.shape[0], dtype=jnp.float32) + 1.0) * 0.5
    radial_basis = jnp.exp(-decays[:, None] * radius_sq[None, :]) * envelope[None, :]
    hidden_one = jax.nn.silu(
        jnp.dot(radial_basis.T, w_basis, precision=lax.Precision.HIGHEST)
    ).astype(jnp.bfloat16)
    hidden_two = jax.nn.silu(
        jnp.dot(hidden_one, w_hidden, preferred_element_type=jnp.float32)
    ).astype(jnp.bfloat16)
    radial = jnp.dot(hidden_two, w_radial, preferred_element_type=jnp.float32).reshape(
        edge_count, 3, channels
    )
    widened = jnp.concatenate(
        [
            radial[:, 0:1],
            jnp.broadcast_to(radial[:, 1:2], (edge_count, 3, channels)),
            jnp.broadcast_to(radial[:, 2:3], (edge_count, 5, channels)),
        ],
        axis=1,
    )
    angular = harmonics(scaled).T
    message = (widened * angular[:, :, None] * sender_rows.astype(jnp.float32)[:, None, :]).astype(
        jnp.bfloat16
    )
    onehot = (slot_ids[None, :] == jnp.arange(RT, dtype=jnp.int32)[:, None]).astype(jnp.bfloat16)
    product = jnp.dot(
        onehot, message.reshape(edge_count, 9 * channels), preferred_element_type=jnp.float32
    )
    return product.reshape(RT, 9, channels)


def atom_energy_of(sums_in, own_rows, w_mix, w_read, w_out):
    scaled_sums = sums_in * sums_scale
    invariants = jnp.concatenate(
        [
            scaled_sums[:, 0],
            jnp.sum(scaled_sums[:, 1:4] ** 2, axis=1),
            jnp.sum(scaled_sums[:, 4:9] ** 2, axis=1),
        ],
        axis=1,
    ).astype(jnp.bfloat16)
    updated = own_rows.astype(jnp.float32) + jnp.dot(
        invariants, w_mix, preferred_element_type=jnp.float32
    )
    readout = jax.nn.silu(jnp.dot(updated, w_read, precision=lax.Precision.HIGHEST))
    return jnp.dot(readout, w_out, precision=lax.Precision.HIGHEST)


def image_shift():
    offsets = jnp.arange(3, dtype=jnp.float32) - 1.0
    grids = jnp.meshgrid(offsets, offsets, offsets, indexing="ij")
    return jnp.stack(grids, axis=-1) * domain_side


def add_block(totals, tile_part, base_row):
    zero_index = base_row * 0
    current = lax.dynamic_slice(totals, (base_row, zero_index, zero_index), tile_part.shape)
    return lax.dynamic_update_slice(totals, current + tile_part, (base_row, zero_index, zero_index))


def shards(
    features,
    positions,
    w_up,
    w_basis,
    w_hidden,
    w_radial,
    w_mix,
    w_read,
    w_out,
    send_lists,
    tile_senders,
    tile_slots,
    tile_bases,
    tile_live,
):
    own_rows = features[0, 0, 0]
    own_coords = positions[0, 0, 0]
    lists_here = send_lists[0, 0, 0]
    named_atoms = lists_here.reshape(-1)
    senders = tile_senders[0, 0, 0]
    slot_table = tile_slots[0, 0, 0]
    base_table = tile_bases[0, 0, 0]
    live_count = tile_live[0, 0, 0]
    atom_count, channels = own_rows.shape
    slot_count = send_lists.shape[-1]
    projected = jnp.dot(own_rows, w_up, preferred_element_type=jnp.float32).astype(jnp.bfloat16)
    out_rows = projected[named_atoms].reshape(3, 3, 3, slot_count, channels)
    out_coords = jnp.moveaxis(own_coords[:, named_atoms].reshape(3, 3, 3, 3, slot_count), 0, 3)
    got_rows = extended(out_rows, (("gx", 0), ("gy", 1), ("gz", 2)), 1)
    got_coords = extended(out_coords, (("gx", 0), ("gy", 1), ("gz", 2)), 1)
    in_rows = got_rows[0::2, 0::2, 0::2].reshape(27 * slot_count, channels)
    in_coords = got_coords[0::2, 0::2, 0::2] + image_shift()[:, :, :, :, None]
    in_coords = jnp.moveaxis(in_coords, 3, 0).reshape(3, 27 * slot_count)
    table_rows = jnp.concatenate([projected, in_rows], axis=0)
    table_coords = jnp.concatenate([own_coords, in_coords], axis=1)

    def tile_inputs(tile_index):
        sender = senders[tile_index]
        slot_ids = slot_table[tile_index]
        base_row = base_table[tile_index]
        receiver = base_row + jnp.minimum(slot_ids, RT - 1)
        separation = table_coords[:, sender] - own_coords[:, receiver]
        return (separation, table_rows[sender], slot_ids, sender, receiver, base_row)

    def tile_work(separation, sender_rows, slot_ids):
        return tile_sums(separation, sender_rows, slot_ids, w_basis, w_hidden, w_radial)

    def forward_tile(tile_index, totals):
        separation, sender_rows, slot_ids, sender, receiver, base_row = tile_inputs(tile_index)
        return add_block(totals, tile_work(separation, sender_rows, slot_ids), base_row)

    totals = lax.fori_loop(
        0, live_count, forward_tile, jnp.zeros((atom_count, 9, channels), jnp.float32)
    )
    energy, energy_pull = jax.vjp(
        lambda sums_in: atom_energy_of(sums_in, own_rows, w_mix, w_read, w_out), totals
    )
    (grad_sums,) = energy_pull(jnp.ones_like(energy))

    def tile_gradient(separation, sender_rows, slot_ids, cotangent):
        _, tile_pull = jax.vjp(lambda moved: tile_work(moved, sender_rows, slot_ids), separation)
        return tile_pull(cotangent)[0]

    def cotangent_at(base_row):
        zero_index = base_row * 0
        return lax.dynamic_slice(grad_sums, (base_row, zero_index, zero_index), (RT, 9, channels))

    def place(grads_in, grad_sep, sender, receiver):
        return grads_in.at[:, sender].add(grad_sep).at[:, receiver].add(-grad_sep)

    def backward_tile(tile_index, grads_in):
        separation, sender_rows, slot_ids, sender, receiver, base_row = tile_inputs(tile_index)
        grad_sep = tile_gradient(separation, sender_rows, slot_ids, cotangent_at(base_row))
        return place(grads_in, grad_sep, sender, receiver)

    grads = jnp.zeros((3, atom_count + 27 * slot_count), jnp.float32)
    grads = lax.fori_loop(0, live_count, backward_tile, grads)
    own_grad = grads[:, :atom_count]
    halo_grad = jnp.moveaxis(grads[:, atom_count:].reshape(3, 3, 3, 3, slot_count), 0, 3)
    came_back = extended(halo_grad, (("gx", 0), ("gy", 1), ("gz", 2)), 1)
    came_back = jnp.moveaxis(came_back[0::2, 0::2, 0::2], 3, 0).reshape(3, 27 * slot_count)
    own_grad = own_grad.at[:, named_atoms].add(came_back)
    return ((-own_grad)[None, None, None], energy[None, None, None])


def solution(mesh):
    return jax.shard_map(
        shards,
        mesh=mesh,
        in_specs=(
            P("gx", "gy", "gz", None, None),
            P("gx", "gy", "gz", None, None),
            P(),
            P(),
            P(),
            P(),
            P(),
            P(),
            P(),
            P("gx", "gy", "gz", None, None, None, None),
            P("gx", "gy", "gz", None, None),
            P("gx", "gy", "gz", None, None),
            P("gx", "gy", "gz", None),
            P("gx", "gy", "gz"),
        ),
        out_specs=(P("gx", "gy", "gz", None, None), P("gx", "gy", "gz", None)),
        check_vma=False,
    )
```

profile of v0, /device:TPU:30, one launch (start us, length us, event | category | flops | bytes accessed | tf_op | source)
XLA Modules:
  0.0 1769.1 jit_solution(7258880895938368752)
XLA Ops:
  2.5 3.9 gather_fusion.7
  6.5 8.5 collective-permute-start.7
  15.1 3.3 gather_fusion.6
  18.7 2.9 collective-permute-start.1
  23.2 4.8 collective-permute-start.2
  28.0 1.9 collective-permute-start.3
  30.0 6.0 collective-permute-start.8
  36.0 1.9 collective-permute-start.9
  38.1 3.2 collective-permute-start.4
  41.3 2.7 collective-permute-start.5
  46.1 3.2 collective-permute-done.5
  49.6 3.3 collective-permute-start.10
  53.0 2.5 collective-permute-start.11
  57.0 3.7 collective-permute-done.10
  60.7 4.3 collective-permute-done.11
  66.1 187.7 %while.20 = (s32[]{:T(128)}, f32[128,9,128]{2,0,1:T(8,128)S(1)}, s32[]{:T(128)}, s32[64]{0:T(128)S(1)}, s32[64,128]{1,0:T(8,128)}, /*index=5*/s32[64,128]{1,0:T(...) while((s32[]{:T(128)}, f32[128,9,128]{2,0,1:T(8,128)S(1)}, ...), condition=%wide.region_2.3_spmd, body=%wide.region_0.2_spmd.sunk | while | flops 11324448 | bytes 2358085 | solution.py:164
  256.2 304.5 %while.21 = (s32[]{:T(128)}, f32[3,1856]{0,1:T(8,128)S(1)}, s32[]{:T(128)}, s32[64,128]{1,0:T(8,128)}, f32[3,1856]{0,1:T(8,128)}, /*index=5*/s32[64]{0:T(128)S(1...) while((s32[]{:T(128)}, f32[3,1856]{0,1:T(8,128)S(1)}, ...), condition=%wide.region_14.15_spmd, body=%wide.region_5.14_spmd.sunk | while | flops 20221216 | bytes 6955952 | solution.py:189
  561.2 1158.1 %collective-permute-start.12 = (f32[1,3,3,3,64]{4,2,1,0,3:T(4,128)S(1)}, f32[1,3,3,3,64]{4,2,1,0,3:T(4,128)S(1)}, u32[]{:S(2)}, u32[]{:S(2)}) collective-permute-start(f32[1,3,3,3,64]{4,2,1,0,3:T(4,128)S(1)} %get-tuple-element.340), channel_id=1, source_target_pairs={{0,32},{32,64},{64,96},{96,128},{128,160},{160,192},{192,224},{224... | collective-permute-start | bytes 20744 | tf_op jit(solution)/shard_map/ppermute | solution.py:21
  1720.8 17.5 collective-permute-start.14
  1738.3 1.9 collective-permute-start.15
  1740.2 6.0 collective-permute-done.15
  1748.3 3.9 collective-permute-start.17
  1752.9 3.4 collective-permute-done.17
  1756.8 11.7 scatter_fusion.2
  (1415 shorter events, 406.0 us)
Async XLA Ops:
  0.6 253.3 %copy-start = (bf16[384,128]{1,0:T(8,128)(2,1)S(1)}, bf16[384,128]{1,0:T(8,128)(2,1)}, u32[]{:S(2)}) copy-start(bf16[384,128]{1,0:T(8,128)(2,1)} %param.24) | copy-start | bytes 294916
  2.5 12.5 copy-start.6
  6.5 23.5 %collective-permute-start.6 = (bf16[1,3,3,64,128]{4,3,2,1,0:T(8,128)(2,1)S(1)}, bf16[1,3,3,64,128]{4,3,2,1,0:T(8,128)(2,1)S(1)}, u32[]{:S(2)}, u32[]{:S(2)}) collective-permute-start(bf16[1,3,3,64,128]{4,3,2,1,0:T(8,128)(2,1)S(1)} %bitcast.241), channel_id=1, source_target_pairs={{0,32},{32,64},{64,96},{96,128},{128,160},{160,192},{192,224},{224... | collective-permute-start | bytes 442376 | tf_op jit(solution)/shard_map/ppermute | solution.py:21
  6.5 23.5 %collective-permute-start.7 = (bf16[1,3,3,64,128]{4,3,2,1,0:T(8,128)(2,1)S(1)}, bf16[1,3,3,64,128]{4,3,2,1,0:T(8,128)(2,1)S(1)}, u32[]{:S(2)}, u32[]{:S(2)}) collective-permute-start(bf16[1,3,3,64,128]{4,3,2,1,0:T(8,128)(2,1)S(1)} %bitcast.240), channel_id=1, source_target_pairs={{32,0},{64,32},{96,64},{128,96},{160,128},{192,160},{224,192},{256... | collective-permute-start | bytes 442376 | tf_op jit(solution)/shard_map/ppermute | solution.py:22
  18.7 4.4 collective-permute-start
  18.7 4.4 collective-permute-start.1
  23.2 14.8 collective-permute-start.2
  28.0 10.0 collective-permute-start.3
  30.0 19.4 %collective-permute-start.8 = (bf16[5,1,3,64,128]{4,3,2,1,0:T(8,128)(2,1)S(1)}, bf16[5,1,3,64,128]{4,3,2,1,0:T(8,128)(2,1)S(1)}, u32[]{:S(2)}, u32[]{:S(2)}) collective-permute-start(bf16[5,1,3,64,128]{4,3,2,1,0:T(8,128)(2,1)S(1)} %get-tuple-element.325), channel_id=1, source_target_pairs={{0,8},{8,16},{16,24},{24,0},{1,9},{9,17},{17,25},{25,1},{2,10},{10... | collective-permute-start | bytes 737288 | tf_op jit(solution)/shard_map/ppermute | solution.py:21
  36.0 13.4 collective-permute-start.9
  38.1 8.0 collective-permute-start.4
  41.3 8.0 collective-permute-start.5
  49.6 11.0 collective-permute-start.10
  53.0 12.0 collective-permute-start.11
  66.1 187.8 %copy-start.3 = (bf16[1,1,1,128,128]{4,3,2,1,0:T(8,128)(2,1)S(1)}, bf16[1,1,1,128,128]{4,3,2,1,0:T(8,128)(2,1)}, u32[]{:S(2)}) copy-start(bf16[1,1,1,128,128]{4,3,2,1,0:T(8,128)(2,1)} %param.18) | copy-start | bytes 98308
  254.0 2.3 copy-start.4
  411.1 1.4 copy-start.11
  523.1 1.4 copy-start.11
  561.2 1158.9 %collective-permute-start.12 = (f32[1,3,3,3,64]{4,2,1,0,3:T(4,128)S(1)}, f32[1,3,3,3,64]{4,2,1,0,3:T(4,128)S(1)}, u32[]{:S(2)}, u32[]{:S(2)}) collective-permute-start(f32[1,3,3,3,64]{4,2,1,0,3:T(4,128)S(1)} %get-tuple-element.340), channel_id=1, source_target_pairs={{0,32},{32,64},{64,96},{96,128},{128,160},{160,192},{192,224},{224... | collective-permute-start | bytes 20744 | tf_op jit(solution)/shard_map/ppermute | solution.py:21
  1719.3 1.5 collective-permute-start.13
  1720.8 19.4 %collective-permute-start.14 = (f32[5,1,3,3,64]{4,3,2,1,0:T(4,128)S(1)}, f32[5,1,3,3,64]{4,3,2,1,0:T(4,128)S(1)}, u32[]{:S(2)}, u32[]{:S(2)}) collective-permute-start(f32[5,1,3,3,64]{4,3,2,1,0:T(4,128)S(1)} %get-tuple-element.336), channel_id=1, source_target_pairs={{0,8},{8,16},{16,24},{24,0},{1,9},{9,17},{17,25},{25,1},{2,10},{10... | collective-permute-start | bytes 34568 | tf_op jit(solution)/shard_map/ppermute | solution.py:21
  1738.3 7.9 collective-permute-start.15
  1746.3 6.6 collective-permute-start.16
  1748.3 8.0 collective-permute-start.17
  (42 other events, 39.3 us)
where the time goes:
time: 1790 us; the launch traced here: 1770 us
  starting transfers between devices  1220 us (68%)
  local copies, waits for them, and re-layouts  211 us (12%)
  other arithmetic  148 us (8%)
  loops' own time  103 us (6%)
  matrix products  59.6 us (3%)
  waiting for transfers between devices  24.8 us (1%)
    ppermute x9, starting transfers between devices, extended(): before = lax.ppermute(last, axis, up)  1190 us
    gather x152, local copies, waits for them, and re-layouts, tile_inputs(): separation = table_coords[:, sender] - own_coords[:, receiver]  99.6 us
    scatter-add x38, other arithmetic, place(): return grads_in.at[:, sender].add(grad_sep).at[:, receiver].add(-grad_sep)  61 us
    another operation x1, loops' own time, shards(): grads = lax.fori_loop(0, live_count, backward_tile, grads)  53.3 us
    another operation x1, loops' own time, shards(): lax.fori_loop(0, live_count, forward_tile, jnp.zeros((atom_count, 9, chan...  50.1 us
    select_n x38, other arithmetic, tile_inputs(): separation = table_coords[:, sender] - own_coords[:, receiver]  38.5 us
  transfers between devices with their start and end apart: 18, of which 10 were waited for; matrix products, arithmetic and copies ran while one was open for 0% of the time, Pallas kernels for 0%

commit v1 on v0

v1 whole, which is shorter than its diff:
```python
import functools

import jax
import jax.numpy as jnp
from jax import lax
from jax.experimental import pallas as pl
from jax.experimental.pallas import tpu as pltpu
from jax.sharding import PartitionSpec as P

MESH = pl.DeviceIdType.MESH
F32 = jnp.float32
BF16 = jnp.bfloat16
I32 = jnp.int32

ATOMS = 128
C = 128
SLOTS = 64
TILES = 64
EDGE = 128
RT = 8
RH = 64
NB = 8
RO = 16
JR = TILES * RT
PE = 2 * EDGE
RP = 2 * RT
PER_STEP = 2
STEPS = TILES // 2 // PER_STEP
ES = PE * PER_STEP
TS = 2 * PER_STEP

SIDE = 11.0
INV_CUT = 0.2
R3 = 3.0**0.5
R5 = 5.0**0.5
R15 = 15.0**0.5
DEGREE = (0, 1, 1, 1, 2, 2, 2, 2, 2)
SPANS = ((0, 1), (1, 4), (4, 9))

DIRS = tuple((b // 9 - 1, b // 3 % 3 - 1, b % 3 - 1) for b in range(27))
NONZERO = tuple(sum(v != 0 for v in d) for d in DIRS)
COUNT = tuple(SLOTS * 2 // 2 ** max(k, 1) for k in NONZERO)
OTHERS = tuple(b for b in range(27) if b != 13)


def groups_of():
    groups = []
    for k in (1, 2, 3):
        here = [b for b in OTHERS if NONZERO[b] == k and b < 13]
        per = ATOMS // (SLOTS * 2 // 2**k) // 2
        for first in range(0, len(here), per):
            some = here[first : first + per]
            groups.append(tuple(some) + tuple(26 - b for b in some))
    return tuple(groups)


GROUPS = groups_of()
NG = len(GROUPS)
BLOCKS = NG + 1
GROUP = {b: g for g, some in enumerate(GROUPS) for b in some}
AT = {b: k * COUNT[b] for some in GROUPS for k, b in enumerate(some)}


def dot(a, b, ca, cb, precision=None):
    return lax.dot_general(
        a, b, (((ca,), (cb,)), ((), ())), preferred_element_type=F32, precision=precision
    )


def iota(shape, dim):
    return lax.broadcasted_iota(I32, shape, dim)


def hot(condition):
    return jnp.where(condition, 1.0, 0.0).astype(BF16)


def sigmoid(x):
    return 0.5 + 0.5 * jnp.tanh(0.5 * x)


def split(x):
    hi = x.astype(BF16)
    return hi, (x - hi.astype(F32)).astype(BF16)


def lanes(row, index):
    return jnp.take_along_axis(jnp.broadcast_to(row, index.shape), index, axis=1)


def kernel(
    sizes,
    feat_hbm,
    pos_hbm,
    wup_hbm,
    wbasis_hbm,
    whid_hbm,
    wrad_hbm,
    wmix_hbm,
    wread_hbm,
    wout_hbm,
    lists_hbm,
    send_hbm,
    slot_hbm,
    base_hbm,
    live_hbm,
    force_ref,
    energy_ref,
    feat_ref,
    pos_ref,
    wup_ref,
    wbasis_ref,
    whid_ref,
    wrad_ref,
    wmix_ref,
    wread_ref,
    wout_ref,
    lists_ref,
    send_ref,
    slot_ref,
    base_ref,
    live_ref,
    stage_sem,
    out_rows,
    out_xyz,
    table_b,
    in_xyz,
    table_t,
    table_c,
    chosen_ref,
    rows_ref,
    g_ref,
    a_ref,
    d1_ref,
    d2_ref,
    p_ref,
    s_ref,
    u_ref,
    rad_ref,
    slots_ref,
    low_ref,
    high_ref,
    target_ref,
    dharm_ref,
    drad_ref,
    gsep_ref,
    acc_ref,
    racc_ref,
    out_grad,
    in_grad,
    wbt_ref,
    wht_ref,
    wrt_ref,
    wb3_ref,
    row_send,
    row_recv,
    xyz_send,
    xyz_recv,
    grad_send,
    grad_recv,
):
    here = tuple(lax.axis_index(name) for name in ("gx", "gy", "gz"))

    def device(b):
        return tuple(lax.rem(c + (d + n), n) for c, d, n in zip(here, DIRS[b], sizes))

    barrier = pltpu.get_barrier_semaphore()
    for b in OTHERS:
        pl.semaphore_signal(barrier, inc=1, device_id=device(b), device_id_type=MESH)

    staged = {}
    moves = (
        ("feat", feat_hbm, feat_ref),
        ("wup", wup_hbm, wup_ref),
        ("lists", lists_hbm, lists_ref),
        ("pos", pos_hbm, pos_ref),
        ("base", base_hbm, base_ref),
        ("live", live_hbm, live_ref),
        ("slot", slot_hbm, slot_ref),
        ("send", send_hbm, send_ref),
        ("wbasis", wbasis_hbm, wbasis_ref),
        ("whid", whid_hbm, whid_ref),
        ("wrad", wrad_hbm, wrad_ref),
        ("wmix", wmix_hbm, wmix_ref),
        ("wread", wread_hbm, wread_ref),
        ("wout", wout_hbm, wout_ref),
    )
    for k, (name, source, target) in enumerate(moves):
        staged[name] = pltpu.make_async_copy(source, target, stage_sem.at[k])
        staged[name].start()
    early = ("feat", "wup", "lists", "pos")
    for name in early:
        staged[name].wait()

    projected = dot(feat_ref[...], wup_ref[...], 1, 0).astype(BF16)
    table_b[0:ATOMS, :] = projected
    own = jnp.concatenate([pos_ref[d] for d in range(3)], axis=0)
    lane = iota((1, 128), 1)
    for g, some in enumerate(GROUPS):
        order = sorted(some, key=lambda b: AT[26 - b])
        named = jnp.concatenate([lists_ref[b][:, 0 : COUNT[b]] for b in order], axis=1)
        chosen = hot(iota((ATOMS, 128), 0) == named)
        chosen_ref[g] = chosen
        out_rows[128 * g : 128 * g + 128, :] = dot(chosen, projected, 0, 0).astype(BF16)
        for d in range(3):
            shift = jnp.zeros((1, 128), F32)
            for b in some:
                if DIRS[b][d]:
                    inside = (lane >= AT[26 - b]) & (lane < AT[26 - b] + COUNT[b])
                    shift = jnp.where(inside, -SIDE * DIRS[b][d], shift)
            moved = lanes(own[d : d + 1, :], jnp.broadcast_to(named, (8, 128)))[0:1, :]
            out_xyz[g, d : d + 1, :] = moved + shift

    pl.semaphore_wait(barrier, 26)

    row_copies, xyz_copies = [], []
    for b in OTHERS:
        n, g, spot = COUNT[b], GROUP[b], AT[26 - b]
        row_copies.append(
            pltpu.make_async_remote_copy(
                src_ref=out_rows.at[pl.ds(128 * g + spot, n), :],
                dst_ref=table_b.at[pl.ds(128 * (g + 1) + spot, n), :],
                send_sem=row_send.at[b],
                recv_sem=row_recv.at[26 - b],
                device_id=device(b),
                device_id_type=MESH,
            )
        )
        xyz_copies.append(
            pltpu.make_async_remote_copy(
                src_ref=out_xyz.at[g],
                dst_ref=in_xyz.at[26 - b],
                send_sem=xyz_send.at[b],
                recv_sem=xyz_recv.at[26 - b],
                device_id=device(b),
                device_id_type=MESH,
            )
        )
    for one, two in zip(row_copies, xyz_copies):
        two.start()
        one.start()

    for name in staged:
        if name not in early:
            staged[name].wait()

    eye = hot(iota((128, 128), 0) == iota((128, 128), 1))
    eye64 = eye[0:64, 0:64]
    wb_hi, wb_lo = split(wbasis_ref[...])
    hi, lo = wb_hi.astype(F32), wb_lo.astype(F32)
    stacked = jnp.concatenate([hi, hi, lo, lo], axis=0).astype(BF16)
    wbt_ref[...] = dot(eye64, stacked, 1, 1).astype(BF16)
    wht_ref[...] = dot(eye64, whid_ref[...], 1, 1).astype(BF16)
    for degree in range(3):
        part = wrad_ref[:, degree * C : degree * C + C]
        wrt_ref[degree * C : degree * C + C, :] = dot(eye, part, 1, 1).astype(BF16)
    wb3_ref[...] = jnp.concatenate([hi, hi, lo], axis=1).astype(BF16)

    base_rows = jnp.broadcast_to(base_ref[...].astype(F32), (128, TILES)).astype(BF16)
    eye_tiles = hot(iota((TILES, TILES), 0) == iota((TILES, TILES), 1))
    base_tiles = dot(eye_tiles, base_rows, 1, 1)
    slots_ref[...] = jnp.where(iota((TILES, EDGE), 0) < live_ref[0, 0], slot_ref[...], RT)
    receiver = base_tiles.astype(I32) + jnp.minimum(slot_ref[...], RT - 1)
    target_ref[...] = receiver

    def place_lanes():
        reach = hot(iota((TILES, JR), 1) // RT == iota((TILES, JR), 0))
        expanded = dot(base_rows, reach, 1, 0).astype(I32) + iota((128, JR), 1) % RT
        return hot(expanded == iota((128, JR), 0))

    def place_rows():
        reach = hot(iota((JR, TILES), 0) // RT == iota((JR, TILES), 1))
        expanded = dot(reach, base_rows, 1, 1).astype(I32) + iota((JR, 128), 0) % RT
        return hot(expanded == iota((JR, 128), 1))

    block_lane = iota((1, 128), 1)
    moved_by = jnp.zeros((1, 128), I32)
    for b in OTHERS:
        offset = 128 * (GROUP[b] + 1) + AT[b] - (ATOMS + b * SLOTS)
        moved_by = jnp.where(block_lane == b + 2, offset, moved_by)
    for g in range(TILES // 8):
        at = slice(8 * g, 8 * g + 8)
        entry = send_ref[at, :]
        entry = entry + lanes(moved_by, jnp.right_shift(entry, 6))
        low_ref[at, :] = jnp.bitwise_and(entry, 127)
        high_ref[at, :] = jnp.right_shift(entry, 7)

    for two in xyz_copies:
        two.wait()
    for d in range(3):
        table_c[0, d : d + 1, :] = own[d : d + 1, :]
    for g, some in enumerate(GROUPS):
        value = in_xyz[some[0], 0:3, :]
        for b in some[1:]:
            value = jnp.where(lane >= AT[b], in_xyz[b, 0:3, :], value)
        table_c[g + 1, 0:3, :] = value

    for g in range(TILES // 8):
        at = slice(8 * g, 8 * g + 8)
        low, high = low_ref[at, :], high_ref[at, :]
        square = None
        for d in range(3):
            value = lanes(table_c[0, d : d + 1, :], low)
            for k in range(1, BLOCKS):
                value = jnp.where(high == k, lanes(table_c[k, d : d + 1, :], low), value)
            u = (value - lanes(own[d : d + 1, :], receiver[at, :])) * INV_CUT
            u_ref[d, at, :] = u
            square = u * u if square is None else square + u * u
        rad_ref[at, :] = square

    for one in row_copies:
        one.wait()
    for k in range(BLOCKS):
        block = table_b[128 * k : 128 * k + 128, :]
        table_t[:, 128 * k : 128 * k + 128] = dot(eye, block, 1, 1).astype(BF16)

    decay = (iota((NB, ES), 0).astype(F32) + 1.0) * 0.5
    slot_ids = iota((RP, PE), 0)
    half_shift = jnp.where(iota((1, PE), 1) < EDGE, 0, RT)
    row_ids = iota((128, PE), 0)

    def tiles_of(ref, first, count):
        return jnp.concatenate([ref[pl.ds(first + k, 1), :] for k in range(count)], axis=1)

    def onehot_of(first):
        pair = tiles_of(slots_ref, first, 2)
        pair = jnp.where(pair < RT, pair + half_shift, RP)
        return jnp.where(slot_ids == pair, 1.0, 0.0)

    def radial_parts(step):
        s = tiles_of(rad_ref, step * TS, TS)
        reach = jnp.maximum(1.0 - s * s, 0.0)
        return s, reach, jnp.exp(-decay * s)

    def forward(step, carry):
        s, reach, fall = radial_parts(step)
        basis = fall * (reach * reach)
        hi = basis.astype(BF16).astype(F32)
        lo = basis - hi
        basis4 = jnp.concatenate([hi, lo, hi, lo], axis=0).astype(BF16)
        pre1 = dot(wbt_ref[...], basis4, 1, 0)
        rows = []
        for q in range(PER_STEP):
            low = tiles_of(low_ref, step * TS + 2 * q, 2)
            high = tiles_of(high_ref, step * TS + 2 * q, 2)
            at_low = hot(row_ids == low)
            total = None
            for k in range(0, BLOCKS, 2):
                both = jnp.concatenate(
                    [at_low * hot(high == k), at_low * hot(high == k + 1)], axis=0
                )
                part = dot(table_t[:, 128 * k : 128 * k + 256], both, 1, 0)
                total = part if total is None else total + part
            rows.append(total)
        sig1 = sigmoid(pre1)
        act1 = pre1 * sig1
        d1_ref[step] = sig1 + act1 * (1.0 - sig1)
        pre2 = dot(wht_ref[...], act1.astype(BF16), 1, 0)
        sig2 = sigmoid(pre2)
        act2 = pre2 * sig2
        d2_ref[step] = sig2 + act2 * (1.0 - sig2)
        act2 = act2.astype(BF16)
        weights = []
        for q in range(PER_STEP):
            first = step * TS + 2 * q
            onehot = onehot_of(first)
            ux, uy, uz = (tiles_of(u_ref.at[d], first, 2) for d in range(3))
            harm = (
                None,
                R3 * ux,
                R3 * uy,
                R3 * uz,
                R15 * ux * uy,
                R15 * uy * uz,
                0.5 * R5 * (2.0 * uz * uz - ux * ux - uy * uy),
                R15 * ux * uz,
                0.5 * R15 * (ux * ux - uy * uy),
            )
            both = jnp.concatenate(
                [onehot if h is None else onehot * h for h in harm], axis=0
            ).astype(BF16)
            a_ref[step * PER_STEP + q] = both
            weights.append(both)
            rows_ref[step * PER_STEP + q] = rows[q]
        for q in range(PER_STEP):
            radial = dot(wrt_ref[...], act2[:, q * PE : q * PE + PE], 1, 0)
            place = pl.ds((step * PER_STEP + q) * RP, RP)
            for degree, (first, last) in enumerate(SPANS):
                g = (radial[degree * C : degree * C + C, :] * rows[q]).astype(BF16)
                g_ref[step * PER_STEP + q, degree * C : degree * C + C, :] = g
                part = dot(weights[q][first * RP : last * RP, :], g, 1, 1).astype(BF16)
                for m in range(first, last):
                    p_ref[place, m * C : m * C + C] = part[
                        (m - first) * RP : (m - first) * RP + RP, :
                    ]
        return carry

    lax.fori_loop(0, STEPS, forward, 0)

    sums = dot(place_lanes(), p_ref[...], 1, 0)
    halves = [0.5 * sums[:, m * C : m * C + C] for m in range(9)]
    inv = [halves[0]]
    for first, last in SPANS[1:]:
        total = halves[first] * halves[first]
        for m in range(first + 1, last):
            total = total + halves[m] * halves[m]
        inv.append(total)
    invariants = jnp.concatenate(inv, axis=1).astype(BF16)
    updated = feat_ref[...].astype(F32) + dot(invariants, wmix_ref[...], 1, 0)
    high = lax.Precision.HIGHEST
    pre = dot(wread_ref[...], updated, 1, 1, high)
    sig = sigmoid(pre)
    act = pre * sig
    row = iota((RO, ATOMS), 0)
    outw = jnp.zeros((RO, ATOMS), F32)
    for r in range(RO):
        outw = jnp.where(row == r, wout_ref[r], outw)
    energy_ref[...] = jnp.sum(outw * act, axis=0, keepdims=True)
    dpre = outw * (sig + act * (1.0 - sig))
    dupd = dot(dpre, wread_ref[...], 0, 0, high)
    dinv = dot(dupd.astype(BF16), wmix_ref[...], 1, 1).astype(BF16).astype(F32)
    grads = []
    for m in range(9):
        part = dinv[:, DEGREE[m] * C : DEGREE[m] * C + C]
        grads.append(0.5 * part if m == 0 else halves[m] * part)
    grads = jnp.concatenate(grads, axis=1).astype(BF16)
    s_ref[...] = dot(place_rows(), grads, 1, 0).astype(BF16)

    def backward(step, carry):
        dradial = []
        for q in range(PER_STEP):
            pair = step * PER_STEP + q
            onehot = onehot_of(step * TS + 2 * q)
            place = pl.ds(pair * RP, RP)
            parts = []
            for degree, (first, last) in enumerate(SPANS):
                cot = jnp.concatenate(
                    [s_ref[place, m * C : m * C + C] for m in range(first, last)], axis=0
                )
                across = slice(degree * C, degree * C + C)
                dg = dot(cot, a_ref[pair, first * RP : last * RP, :], 0, 0)
                parts.append((dg * rows_ref[pair]).astype(BF16))
                if degree:
                    back = dot(cot, g_ref[pair, across, :], 1, 0)
                    for m in range(first, last):
                        one = back[(m - first) * RP : (m - first) * RP + RP, :]
                        dh = jnp.sum(one * onehot, axis=0, keepdims=True)
                        dharm_ref[m, pl.ds(2 * pair, 1), :] = dh[:, 0:EDGE]
                        dharm_ref[m, pl.ds(2 * pair + 1, 1), :] = dh[:, EDGE:PE]
            dradial.append(jnp.concatenate(parts, axis=0))
        dact2 = dot(wrad_ref[...], jnp.concatenate(dradial, axis=1), 1, 0)
        dpre2 = (dact2 * d2_ref[step]).astype(BF16)
        dact1 = dot(whid_ref[...], dpre2, 1, 0)
        dpre1 = dact1 * d1_ref[step]
        hi, lo = split(dpre1)
        dbasis = dot(wb3_ref[...], jnp.concatenate([hi, lo, hi], axis=0), 1, 0)
        s, reach, fall = radial_parts(step)
        slope = fall * (-decay * (reach * reach) - (4.0 * s) * reach)
        ds = jnp.sum(dbasis * slope, axis=0, keepdims=True)
        for k in range(TS):
            drad_ref[pl.ds(step * TS + k, 1), :] = ds[:, k * EDGE : k * EDGE + EDGE]
        return carry

    lax.fori_loop(0, STEPS, backward, 0)

    ux, uy, uz = u_ref[0], u_ref[1], u_ref[2]
    twice = 2.0 * drad_ref[...]
    dh = [None] + [dharm_ref[m] for m in range(1, 9)]
    gx = twice * ux + R3 * dh[1] + R15 * (uy * dh[4] + uz * dh[7] + ux * dh[8]) - R5 * (ux * dh[6])
    gy = twice * uy + R3 * dh[2] + R15 * (ux * dh[4] + uz * dh[5] - uy * dh[8]) - R5 * (uy * dh[6])
    gz = twice * uz + R3 * dh[3] + R15 * (uy * dh[5] + ux * dh[7]) + (2.0 * R5) * (uz * dh[6])
    gsep_ref[0] = gx * INV_CUT
    gsep_ref[1] = gy * INV_CUT
    gsep_ref[2] = gz * INV_CUT

    acc_ref[...] = jnp.zeros_like(acc_ref)
    racc_ref[...] = jnp.zeros_like(racc_ref)

    def scatter(step, carry):
        for q in range(PER_STEP):
            first = step * TS + 2 * q
            at_low = hot(row_ids == tiles_of(low_ref, first, 2))
            at_target = hot(row_ids == tiles_of(target_ref, first, 2))
            at_high = iota((8, PE), 0) == tiles_of(high_ref, first, 2)
            left, flat = [], []
            for d in range(3):
                g = tiles_of(gsep_ref.at[d], first, 2)
                hi = g.astype(BF16).astype(F32)
                lo = g - hi
                left += [jnp.where(at_high, hi, 0.0), jnp.where(at_high, lo, 0.0)]
                flat += [hi, lo]
            left = jnp.concatenate(left, axis=0).astype(BF16)
            row8 = iota((8, PE), 0)
            stack = jnp.zeros((8, PE), F32)
            for k, value in enumerate(flat):
                stack = jnp.where(row8 == k, value, stack)
            acc_ref[...] += dot(left, at_low, 1, 1)
            racc_ref[...] += dot(stack.astype(BF16), at_target, 1, 1)
        return carry

    lax.fori_loop(0, STEPS, scatter, 0)

    for d in range(3):
        grid = acc_ref[16 * d : 16 * d + 8, :] + acc_ref[16 * d + 8 : 16 * d + 16, :]
        for g in range(NG):
            out_grad[g, d : d + 1, :] = grid[g + 1 : g + 2, :]
        mine = racc_ref[2 * d : 2 * d + 1, :] + racc_ref[2 * d + 1 : 2 * d + 2, :]
        force_ref[d] = mine - grid[0:1, :]

    grad_copies = []
    for b in OTHERS:
        copy = pltpu.make_async_remote_copy(
            src_ref=out_grad.at[GROUP[b]],
            dst_ref=in_grad.at[26 - b],
            send_sem=grad_send.at[b],
            recv_sem=grad_recv.at[26 - b],
            device_id=device(b),
            device_id_type=MESH,
        )
        copy.start()
        grad_copies.append(copy)
    for copy in grad_copies:
        copy.wait()

    total = jnp.zeros((8, ATOMS), F32)
    row8 = iota((8, 128), 0)
    for g, some in enumerate(GROUPS):
        order = sorted(some, key=lambda b: AT[26 - b])
        came = in_grad[order[0]]
        for b in order[1:]:
            came = jnp.where(lane >= AT[26 - b], in_grad[b], came)
        hi, lo = split(jnp.where(row8 < 3, came, 0.0))
        total = total + dot(hi, chosen_ref[g], 1, 1) + dot(lo, chosen_ref[g], 1, 1)
    for d in range(3):
        force_ref[d] = force_ref[d] - total[d : d + 1, :]


def solution(mesh):
    sizes = tuple(mesh.shape[name] for name in ("gx", "gy", "gz"))
    vmem = pl.BlockSpec(memory_space=pltpu.VMEM)
    hbm = pl.BlockSpec(memory_space=pltpu.HBM)
    pairs = TILES // 2

    def step(
        features,
        positions,
        w_up,
        w_basis,
        w_hidden,
        w_radial,
        w_mix,
        w_read,
        w_out,
        send_lists,
        tile_senders,
        tile_slots,
        tile_bases,
        tile_live,
    ):
        dma = pltpu.SemaphoreType.DMA((27,))
        force, energy = pl.pallas_call(
            functools.partial(kernel, sizes),
            out_shape=(
                jax.ShapeDtypeStruct((3, 1, ATOMS), F32),
                jax.ShapeDtypeStruct((1, ATOMS), F32),
            ),
            in_specs=[hbm] * 14,
            out_specs=(vmem, vmem),
            scratch_shapes=[
                pltpu.VMEM((ATOMS, C), BF16),
                pltpu.VMEM((3, 1, ATOMS), F32),
                pltpu.VMEM((C, C), BF16),
                pltpu.VMEM((NB, RH), F32),
                pltpu.VMEM((RH, RH), BF16),
                pltpu.VMEM((RH, 3 * C), BF16),
                pltpu.VMEM((3 * C, C), BF16),
                pltpu.VMEM((RO, C), F32),
                pltpu.SMEM((RO,), F32),
                pltpu.VMEM((27, 1, SLOTS), I32),
                pltpu.VMEM((TILES, EDGE), I32),
                pltpu.VMEM((TILES, EDGE), I32),
                pltpu.VMEM((1, TILES), I32),
                pltpu.SMEM((1, 1), I32),
                pltpu.SemaphoreType.DMA((14,)),
                pltpu.VMEM((NG * 128, C), BF16),
                pltpu.VMEM((NG, 8, 128), F32),
                pltpu.VMEM((BLOCKS * 128, C), BF16),
                pltpu.VMEM((27, 8, 128), F32),
                pltpu.VMEM((C, BLOCKS * 128), BF16),
                pltpu.VMEM((BLOCKS, 8, 128), F32),
                pltpu.VMEM((NG, ATOMS, 128), BF16),
                pltpu.VMEM((pairs, C, PE), F32),
                pltpu.VMEM((pairs, 3 * C, PE), BF16),
                pltpu.VMEM((pairs, 9 * RP, PE), BF16),
                pltpu.VMEM((STEPS, RH, ES), F32),
                pltpu.VMEM((STEPS, RH, ES), F32),
                pltpu.VMEM((JR, 9 * C), BF16),
                pltpu.VMEM((JR, 9 * C), BF16),
                pltpu.VMEM((3, TILES, EDGE), F32),
                pltpu.VMEM((TILES, EDGE), F32),
                pltpu.VMEM((TILES, EDGE), I32),
                pltpu.VMEM((TILES, EDGE), I32),
                pltpu.VMEM((TILES, EDGE), I32),
                pltpu.VMEM((TILES, EDGE), I32),
                pltpu.VMEM((9, TILES, EDGE), F32),
                pltpu.VMEM((TILES, EDGE), F32),
                pltpu.VMEM((3, TILES, EDGE), F32),
                pltpu.VMEM((48, 128), F32),
                pltpu.VMEM((8, 128), F32),
                pltpu.VMEM((NG, 8, 128), F32),
                pltpu.VMEM((27, 8, 128), F32),
                pltpu.VMEM((RH, 4 * NB), BF16),
                pltpu.VMEM((RH, RH), BF16),
                pltpu.VMEM((3 * C, RH), BF16),
                pltpu.VMEM((NB, 3 * RH), BF16),
                dma,
                dma,
                dma,
                dma,
                dma,
                dma,
            ],
            compiler_params=pltpu.CompilerParams(
                collective_id=0,
                has_side_effects=True,
                vmem_limit_bytes=64 * 2**20 - 65536,
            ),
        )(
            features.reshape(ATOMS, C),
            positions.reshape(3, 1, ATOMS),
            w_up,
            w_basis,
            w_hidden,
            w_radial,
            w_mix,
            w_read.T,
            w_out,
            send_lists.reshape(27, 1, SLOTS),
            tile_senders.reshape(TILES, EDGE),
            tile_slots.reshape(TILES, EDGE),
            tile_bases.reshape(1, TILES),
            tile_live.reshape(1, 1),
        )
        return force.reshape(1, 1, 1, 3, ATOMS), energy.reshape(1, 1, 1, ATOMS)

    cube = ("gx", "gy", "gz")
    return jax.shard_map(
        step,
        mesh=mesh,
        in_specs=(
            P(*cube, None, None),
            P(*cube, None, None),
            P(),
            P(),
            P(),
            P(),
            P(),
            P(),
            P(),
            P(*cube, None, None, None, None),
            P(*cube, None, None),
            P(*cube, None, None),
            P(*cube, None),
            P(*cube),
        ),
        out_specs=(P(*cube, None, None), P(*cube, None)),
        check_vma=False,
    )
```

time: 1790 us -> 67.6 us (0.04)
  the two profiles are of different devices: /device:TPU:30 before, /device:TPU:16 now
where the time goes in v1:
time: 67.6 us; the launch traced here: 67.4 us
  Pallas kernels  64.3 us (95%)
  local copies, waits for them, and re-layouts  1.8 us (3%)
  between operations  1.3 us (2%)
    pallas_call x1, Pallas kernels, step(): pl.pallas_call(functools.partial(kernel, sizes), out_shape=(jax.ShapeDtyp...  64.3 us
    unnamed x6, local copies, waits for them, and re-layouts  1.8 us

profile of v1, /device:TPU:16, one launch (start us, length us, event | category | flops | bytes accessed | tf_op | source)
XLA Modules:
  0.0 67.4 jit_solution(18388590318983421445)
XLA Ops:
  1.3 64.3 %shard_map.149 = (f32[3,1,128]{2,1,0:T(1,128)}, f32[1,128]{1,0:T(1,128)}) custom-call(bf16[128,128]{1,0:T(8,128)(2,1)} %bitcast.13, f32[3,1,128]{2,1,0:T(1,128)} %bitcast.18, bf16[128,128]{1,0:T(8,128)(2,1)} %wup_hbm.1, f32[8,64]{1,0:T(8,128)} %wbasis_hbm.1, bf16[64,64]{1,0:T(8,128)(2,1)} %whid_hbm.1, bf16[64,384]{1,0:T(8,128)(2,1)} %wrad_hbm.1, ...), custom_call_target="tpu_custom_call" | custom-call | tf_op jit(solution)/shard_map/pallas_call | solution.py:561
  65.6 0.0 copy-start
  65.6 0.7 copy-done
  66.2 0.0 copy-start.1
  66.2 0.6 copy.20
  66.8 0.1 copy-done.1
  66.9 0.5 copy.21
Async XLA Ops:
  65.6 0.7 copy-start
  66.2 0.6 copy-start.1

commit v2 on v1

--- a/solution.py
+++ b/solution.py
@@ -24,7 +24,7 @@
 JR = TILES * RT
 PE = 2 * EDGE
 RP = 2 * RT
-PER_STEP = 2
+PER_STEP = 4
 STEPS = TILES // 2 // PER_STEP
 ES = PE * PER_STEP
 TS = 2 * PER_STEP
@@ -128,8 +128,11 @@
     table_t,
     table_c,
     chosen_ref,
+    at_ref,
+    h2_ref,
     rows_ref,
     g_ref,
+    dr_ref,
     a_ref,
     d1_ref,
     d2_ref,
@@ -137,6 +140,7 @@
     s_ref,
     u_ref,
     rad_ref,
+    harm_ref,
     slots_ref,
     low_ref,
     high_ref,
@@ -298,15 +302,29 @@
     for g in range(TILES // 8):
         at = slice(8 * g, 8 * g + 8)
         low, high = low_ref[at, :], high_ref[at, :]
-        square = None
+        parts = []
         for d in range(3):
             value = lanes(table_c[0, d : d + 1, :], low)
             for k in range(1, BLOCKS):
                 value = jnp.where(high == k, lanes(table_c[k, d : d + 1, :], low), value)
             u = (value - lanes(own[d : d + 1, :], receiver[at, :])) * INV_CUT
             u_ref[d, at, :] = u
-            square = u * u if square is None else square + u * u
-        rad_ref[at, :] = square
+            parts.append(u)
+        ux, uy, uz = parts
+        xx, yy, zz = ux * ux, uy * uy, uz * uz
+        rad_ref[at, :] = xx + yy + zz
+        values = (
+            R3 * ux,
+            R3 * uy,
+            R3 * uz,
+            R15 * ux * uy,
+            R15 * uy * uz,
+            0.5 * R5 * (2.0 * zz - xx - yy),
+            R15 * ux * uz,
+            0.5 * R15 * (xx - yy),
+        )
+        for m, value in enumerate(values):
+            harm_ref[m, at, :] = value
 
     for one in row_copies:
         one.wait()
@@ -314,10 +332,11 @@
         block = table_b[128 * k : 128 * k + 128, :]
         table_t[:, 128 * k : 128 * k + 128] = dot(eye, block, 1, 1).astype(BF16)
 
-    decay = (iota((NB, ES), 0).astype(F32) + 1.0) * 0.5
+    decay = (iota((NB, PE), 0).astype(F32) + 1.0) * 0.5
     slot_ids = iota((RP, PE), 0)
     half_shift = jnp.where(iota((1, PE), 1) < EDGE, 0, RT)
     row_ids = iota((128, PE), 0)
+    inner = range(PER_STEP)
 
     def tiles_of(ref, first, count):
         return jnp.concatenate([ref[pl.ds(first + k, 1), :] for k in range(count)], axis=1)
@@ -327,75 +346,75 @@
         pair = jnp.where(pair < RT, pair + half_shift, RP)
         return jnp.where(slot_ids == pair, 1.0, 0.0)
 
-    def radial_parts(step):
-        s = tiles_of(rad_ref, step * TS, TS)
+    def radial_parts(pair):
+        s = tiles_of(rad_ref, 2 * pair, 2)
         reach = jnp.maximum(1.0 - s * s, 0.0)
         return s, reach, jnp.exp(-decay * s)
 
-    def forward(step, carry):
-        s, reach, fall = radial_parts(step)
-        basis = fall * (reach * reach)
-        hi = basis.astype(BF16).astype(F32)
-        lo = basis - hi
-        basis4 = jnp.concatenate([hi, lo, hi, lo], axis=0).astype(BF16)
-        pre1 = dot(wbt_ref[...], basis4, 1, 0)
-        rows = []
-        for q in range(PER_STEP):
-            low = tiles_of(low_ref, step * TS + 2 * q, 2)
-            high = tiles_of(high_ref, step * TS + 2 * q, 2)
-            at_low = hot(row_ids == low)
-            total = None
-            for k in range(0, BLOCKS, 2):
-                both = jnp.concatenate(
-                    [at_low * hot(high == k), at_low * hot(high == k + 1)], axis=0
-                )
-                part = dot(table_t[:, 128 * k : 128 * k + 256], both, 1, 0)
-                total = part if total is None else total + part
-            rows.append(total)
-        sig1 = sigmoid(pre1)
-        act1 = pre1 * sig1
-        d1_ref[step] = sig1 + act1 * (1.0 - sig1)
-        pre2 = dot(wht_ref[...], act1.astype(BF16), 1, 0)
-        sig2 = sigmoid(pre2)
-        act2 = pre2 * sig2
-        d2_ref[step] = sig2 + act2 * (1.0 - sig2)
-        act2 = act2.astype(BF16)
-        weights = []
-        for q in range(PER_STEP):
-            first = step * TS + 2 * q
-            onehot = onehot_of(first)
-            ux, uy, uz = (tiles_of(u_ref.at[d], first, 2) for d in range(3))
-            harm = (
-                None,
-                R3 * ux,
-                R3 * uy,
-                R3 * uz,
-                R15 * ux * uy,
-                R15 * uy * uz,
-                0.5 * R5 * (2.0 * uz * uz - ux * ux - uy * uy),
-                R15 * ux * uz,
-                0.5 * R15 * (ux * ux - uy * uy),
-            )
-            both = jnp.concatenate(
-                [onehot if h is None else onehot * h for h in harm], axis=0
-            ).astype(BF16)
-            a_ref[step * PER_STEP + q] = both
-            weights.append(both)
-            rows_ref[step * PER_STEP + q] = rows[q]
-        for q in range(PER_STEP):
-            radial = dot(wrt_ref[...], act2[:, q * PE : q * PE + PE], 1, 0)
-            place = pl.ds((step * PER_STEP + q) * RP, RP)
+    def gather(pair):
+        low = tiles_of(low_ref, 2 * pair, 2)
+        high = tiles_of(high_ref, 2 * pair, 2)
+        at_low = hot(row_ids == low)
+        at_ref[pair] = at_low
+        entries = jnp.concatenate([at_low * hot(high == k) for k in range(BLOCKS)], axis=0)
+        rows_ref[pair] = dot(table_t[...], entries, 1, 0).astype(BF16)
+
+    def network(step):
+        pairs = [step * PER_STEP + q for q in inner]
+        basis4 = []
+        for pair in pairs:
+            s, reach, fall = radial_parts(pair)
+            basis = fall * (reach * reach)
+            hi = basis.astype(BF16).astype(F32)
+            lo = basis - hi
+            basis4.append(jnp.concatenate([hi, lo, hi, lo], axis=0).astype(BF16))
+        pre1 = [dot(wbt_ref[...], value, 1, 0) for value in basis4]
+        for pair in pairs[: PER_STEP // 2]:
+            gather(pair)
+        act1 = []
+        for pair, pre in zip(pairs, pre1):
+            sig = sigmoid(pre)
+            act = pre * sig
+            d1_ref[pair] = sig + act * (1.0 - sig)
+            act1.append(act.astype(BF16))
+        pre2 = [dot(wht_ref[...], value, 1, 0) for value in act1]
+        for pair in pairs[PER_STEP // 2 :]:
+            gather(pair)
+        for pair, pre in zip(pairs, pre2):
+            sig = sigmoid(pre)
+            act = pre * sig
+            d2_ref[pair] = sig + act * (1.0 - sig)
+            h2_ref[pair] = act.astype(BF16)
+
+    def gathered(step):
+        for q in inner:
+            pair = step * PER_STEP + q
+            onehot = onehot_of(2 * pair)
+            weights = [onehot]
+            for m in range(8):
+                weights.append(onehot * tiles_of(harm_ref.at[m], 2 * pair, 2))
+            weights = jnp.concatenate(weights, axis=0).astype(BF16)
+            a_ref[pair] = weights
+            rows = rows_ref[pair]
+            place = pl.ds(pair * RP, RP)
+            radial = dot(wrt_ref[...], h2_ref[pair], 1, 0).astype(BF16)
             for degree, (first, last) in enumerate(SPANS):
-                g = (radial[degree * C : degree * C + C, :] * rows[q]).astype(BF16)
-                g_ref[step * PER_STEP + q, degree * C : degree * C + C, :] = g
-                part = dot(weights[q][first * RP : last * RP, :], g, 1, 1).astype(BF16)
+                across = slice(degree * C, degree * C + C)
+                g = radial[across, :] * rows
+                g_ref[pair, across, :] = g
+                part = dot(weights[first * RP : last * RP, :], g, 1, 1).astype(BF16)
                 for m in range(first, last):
                     p_ref[place, m * C : m * C + C] = part[
                         (m - first) * RP : (m - first) * RP + RP, :
                     ]
+
+    def forward(step, carry):
+        gathered(lax.rem(step + (STEPS - 1), STEPS))
+        network(step)
         return carry
 
     lax.fori_loop(0, STEPS, forward, 0)
+    gathered(STEPS - 1)
 
     sums = dot(place_lanes(), p_ref[...], 1, 0)
     halves = [0.5 * sums[:, m * C : m * C + C] for m in range(9)]
@@ -426,20 +445,22 @@
     grads = jnp.concatenate(grads, axis=1).astype(BF16)
     s_ref[...] = dot(place_rows(), grads, 1, 0).astype(BF16)
 
-    def backward(step, carry):
-        dradial = []
-        for q in range(PER_STEP):
+    acc_ref[...] = jnp.zeros_like(acc_ref)
+    racc_ref[...] = jnp.zeros_like(racc_ref)
+
+    def to_edges(step):
+        for q in inner:
             pair = step * PER_STEP + q
-            onehot = onehot_of(step * TS + 2 * q)
+            onehot = onehot_of(2 * pair)
             place = pl.ds(pair * RP, RP)
-            parts = []
+            rows = rows_ref[pair]
             for degree, (first, last) in enumerate(SPANS):
                 cot = jnp.concatenate(
                     [s_ref[place, m * C : m * C + C] for m in range(first, last)], axis=0
                 )
                 across = slice(degree * C, degree * C + C)
                 dg = dot(cot, a_ref[pair, first * RP : last * RP, :], 0, 0)
-                parts.append((dg * rows_ref[pair]).astype(BF16))
+                dr_ref[pair, across, :] = dg.astype(BF16) * rows
                 if degree:
                     back = dot(cot, g_ref[pair, across, :], 1, 0)
                     for m in range(first, last):
@@ -447,58 +468,59 @@
                         dh = jnp.sum(one * onehot, axis=0, keepdims=True)
                         dharm_ref[m, pl.ds(2 * pair, 1), :] = dh[:, 0:EDGE]
                         dharm_ref[m, pl.ds(2 * pair + 1, 1), :] = dh[:, EDGE:PE]
-            dradial.append(jnp.concatenate(parts, axis=0))
-        dact2 = dot(wrad_ref[...], jnp.concatenate(dradial, axis=1), 1, 0)
-        dpre2 = (dact2 * d2_ref[step]).astype(BF16)
-        dact1 = dot(whid_ref[...], dpre2, 1, 0)
-        dpre1 = dact1 * d1_ref[step]
-        hi, lo = split(dpre1)
-        dbasis = dot(wb3_ref[...], jnp.concatenate([hi, lo, hi], axis=0), 1, 0)
-        s, reach, fall = radial_parts(step)
-        slope = fall * (-decay * (reach * reach) - (4.0 * s) * reach)
-        ds = jnp.sum(dbasis * slope, axis=0, keepdims=True)
-        for k in range(TS):
-            drad_ref[pl.ds(step * TS + k, 1), :] = ds[:, k * EDGE : k * EDGE + EDGE]
+
+    def to_radius(step):
+        pairs = [step * PER_STEP + q for q in inner]
+        dact2 = [dot(wrad_ref[...], dr_ref[pair], 1, 0) for pair in pairs]
+        dpre2 = [(value * d2_ref[pair]).astype(BF16) for value, pair in zip(dact2, pairs)]
+        dact1 = [dot(whid_ref[...], value, 1, 0) for value in dpre2]
+        stacks = []
+        for value, pair in zip(dact1, pairs):
+            hi, lo = split(value * d1_ref[pair])
+            stacks.append(jnp.concatenate([hi, lo, hi], axis=0))
+        dbasis = [dot(wb3_ref[...], value, 1, 0) for value in stacks]
+        for value, pair in zip(dbasis, pairs):
+            s, reach, fall = radial_parts(pair)
+            slope = fall * (-decay * (reach * reach) - (4.0 * s) * reach)
+            ds = jnp.sum(value * slope, axis=0, keepdims=True)
+            drad_ref[pl.ds(2 * pair, 1), :] = ds[:, 0:EDGE]
+            drad_ref[pl.ds(2 * pair + 1, 1), :] = ds[:, EDGE:PE]
+
+    def scatter(step, counts):
+        at = pl.ds(pl.multiple_of(step * TS, TS), TS)
+        ux, uy, uz = u_ref[0, at, :], u_ref[1, at, :], u_ref[2, at, :]
+        twice = 2.0 * drad_ref[at, :]
+        dh = [None] + [dharm_ref[m, at, :] for m in range(1, 9)]
+        gx = R3 * dh[1] + R15 * (uy * dh[4] + uz * dh[7] + ux * dh[8]) - R5 * (ux * dh[6])
+        gy = R3 * dh[2] + R15 * (ux * dh[4] + uz * dh[5] - uy * dh[8]) - R5 * (uy * dh[6])
+        gz = R3 * dh[3] + R15 * (uy * dh[5] + ux * dh[7]) + (2.0 * R5) * (uz * dh[6])
+        for d, value in enumerate((twice * ux + gx, twice * uy + gy, twice * uz + gz)):
+            g = jnp.where(counts, value * INV_CUT, 0.0)
+            hi = g.astype(BF16).astype(F32)
+            gsep_ref[2 * d] = hi
+            gsep_ref[2 * d + 1] = g - hi
+        at_high = iota((8, ES), 0) == tiles_of(high_ref, step * TS, TS)
+        at_target = hot(iota((128, ES), 0) == tiles_of(target_ref, step * TS, TS))
+        at_low = jnp.concatenate([at_ref[step * PER_STEP + q] for q in inner], axis=1)
+        row8 = iota((8, ES), 0)
+        left, stack = [], jnp.zeros((8, ES), F32)
+        for k in range(6):
+            value = tiles_of(gsep_ref.at[k], 0, TS)
+            left.append(jnp.where(at_high, value, 0.0))
+            stack = jnp.where(row8 == k, value, stack)
+        acc_ref[...] += dot(jnp.concatenate(left, axis=0).astype(BF16), at_low, 1, 1)
+        racc_ref[...] += dot(stack.astype(BF16), at_target, 1, 1)
+
+    def backward(step, carry):
+        scatter(lax.rem(step + (STEPS - 2), STEPS), step >= 2)
+        to_radius(lax.rem(step + (STEPS - 1), STEPS))
+        to_edges(step)
         return carry
 
     lax.fori_loop(0, STEPS, backward, 0)
-
-    ux, uy, uz = u_ref[0], u_ref[1], u_ref[2]
-    twice = 2.0 * drad_ref[...]
-    dh = [None] + [dharm_ref[m] for m in range(1, 9)]
-    gx = twice * ux + R3 * dh[1] + R15 * (uy * dh[4] + uz * dh[7] + ux * dh[8]) - R5 * (ux * dh[6])
-    gy = twice * uy + R3 * dh[2] + R15 * (ux * dh[4] + uz * dh[5] - uy * dh[8]) - R5 * (uy * dh[6])
-    gz = twice * uz + R3 * dh[3] + R15 * (uy * dh[5] + ux * dh[7]) + (2.0 * R5) * (uz * dh[6])
-    gsep_ref[0] = gx * INV_CUT
-    gsep_ref[1] = gy * INV_CUT
-    gsep_ref[2] = gz * INV_CUT
-
-    acc_ref[...] = jnp.zeros_like(acc_ref)
-    racc_ref[...] = jnp.zeros_like(racc_ref)
-
-    def scatter(step, carry):
-        for q in range(PER_STEP):
-            first = step * TS + 2 * q
-            at_low = hot(row_ids == tiles_of(low_ref, first, 2))
-            at_target = hot(row_ids == tiles_of(target_ref, first, 2))
-            at_high = iota((8, PE), 0) == tiles_of(high_ref, first, 2)
-            left, flat = [], []
-            for d in range(3):
-                g = tiles_of(gsep_ref.at[d], first, 2)
-                hi = g.astype(BF16).astype(F32)
-                lo = g - hi
-                left += [jnp.where(at_high, hi, 0.0), jnp.where(at_high, lo, 0.0)]
-                flat += [hi, lo]
-            left = jnp.concatenate(left, axis=0).astype(BF16)
-            row8 = iota((8, PE), 0)
-            stack = jnp.zeros((8, PE), F32)
-            for k, value in enumerate(flat):
-                stack = jnp.where(row8 == k, value, stack)
-            acc_ref[...] += dot(left, at_low, 1, 1)
-            racc_ref[...] += dot(stack.astype(BF16), at_target, 1, 1)
-        return carry
-
-    lax.fori_loop(0, STEPS, scatter, 0)
+    scatter(STEPS - 2, True)
+    to_radius(STEPS - 1)
+    scatter(STEPS - 1, True)
 
     for d in range(3):
         grid = acc_ref[16 * d : 16 * d + 8, :] + acc_ref[16 * d + 8 : 16 * d + 16, :]
@@ -589,22 +611,26 @@
                 pltpu.VMEM((C, BLOCKS * 128), BF16),
                 pltpu.VMEM((BLOCKS, 8, 128), F32),
                 pltpu.VMEM((NG, ATOMS, 128), BF16),
-                pltpu.VMEM((pairs, C, PE), F32),
+                pltpu.VMEM((pairs, 128, PE), BF16),
+                pltpu.VMEM((pairs, RH, PE), BF16),
+                pltpu.VMEM((pairs, C, PE), BF16),
+                pltpu.VMEM((pairs, 3 * C, PE), BF16),
                 pltpu.VMEM((pairs, 3 * C, PE), BF16),
                 pltpu.VMEM((pairs, 9 * RP, PE), BF16),
-                pltpu.VMEM((STEPS, RH, ES), F32),
-                pltpu.VMEM((STEPS, RH, ES), F32),
+                pltpu.VMEM((pairs, RH, PE), F32),
+                pltpu.VMEM((pairs, RH, PE), F32),
                 pltpu.VMEM((JR, 9 * C), BF16),
                 pltpu.VMEM((JR, 9 * C), BF16),
                 pltpu.VMEM((3, TILES, EDGE), F32),
                 pltpu.VMEM((TILES, EDGE), F32),
+                pltpu.VMEM((8, TILES, EDGE), F32),
                 pltpu.VMEM((TILES, EDGE), I32),
                 pltpu.VMEM((TILES, EDGE), I32),
                 pltpu.VMEM((TILES, EDGE), I32),
                 pltpu.VMEM((TILES, EDGE), I32),
                 pltpu.VMEM((9, TILES, EDGE), F32),
                 pltpu.VMEM((TILES, EDGE), F32),
-                pltpu.VMEM((3, TILES, EDGE), F32),
+                pltpu.VMEM((6, TS, EDGE), F32),
                 pltpu.VMEM((48, 128), F32),
                 pltpu.VMEM((8, 128), F32),
                 pltpu.VMEM((NG, 8, 128), F32),

time: 67.6 us -> 57.7 us (0.85)
  the two profiles are of different devices: /device:TPU:16 before, /device:TPU:8 now
where the time goes in v2:
time: 57.7 us; the launch traced here: 57.5 us
  Pallas kernels  54.3 us (94%)
  local copies, waits for them, and re-layouts  1.8 us (3%)
  between operations  1.3 us (2%)
    pallas_call x1, Pallas kernels, step(): pl.pallas_call(functools.partial(kernel, sizes), out_shape=(jax.ShapeDtyp...  54.3 us
    unnamed x6, local copies, waits for them, and re-layouts  1.8 us

profile of v2, /device:TPU:8, one launch (start us, length us, event | category | flops | bytes accessed | tf_op | source)
XLA Modules:
  0.0 57.5 jit_solution(14622333837889292792)
XLA Ops:
  1.3 54.3 %shard_map.149 = (f32[3,1,128]{2,1,0:T(1,128)}, f32[1,128]{1,0:T(1,128)}) custom-call(bf16[128,128]{1,0:T(8,128)(2,1)} %bitcast.13, f32[3,1,128]{2,1,0:T(1,128)} %bitcast.18, bf16[128,128]{1,0:T(8,128)(2,1)} %wup_hbm.1, f32[8,64]{1,0:T(8,128)} %wbasis_hbm.1, bf16[64,64]{1,0:T(8,128)(2,1)} %whid_hbm.1, bf16[64,384]{1,0:T(8,128)(2,1)} %wrad_hbm.1, ...), custom_call_target="tpu_custom_call" | custom-call | tf_op jit(solution)/shard_map/pallas_call | solution.py:583
  55.6 0.0 copy-start
  55.6 0.7 %copy-done = f32[3,1,128]{2,1,0:T(1,128)S(1)} copy-done((f32[3,1,128]{2,1,0:T(1,128)S(1)}, f32[3,1,128]{2,1,0:T(1,128)}, u32[]{:S(2)}) %copy-start) | copy-done | bytes 1560
  56.3 0.0 copy-start.1
  56.3 0.6 copy.20
  56.9 0.1 copy-done.1
  56.9 0.5 copy.21
Async XLA Ops:
  55.6 0.7 %copy-start = (f32[3,1,128]{2,1,0:T(1,128)S(1)}, f32[3,1,128]{2,1,0:T(1,128)}, u32[]{:S(2)}) copy-start(f32[3,1,128]{2,1,0:T(1,128)} %get-tuple-element.4) | copy-start | bytes 4612
  56.3 0.6 %copy-start.1 = (f32[1,128]{1,0:T(1,128)S(1)}, f32[1,128]{1,0:T(1,128)}, u32[]{:S(2)}) copy-start(f32[1,128]{1,0:T(1,128)} %get-tuple-element.5) | copy-start | bytes 1540

commit v3 on v2

--- a/solution.py
+++ b/solution.py
@@ -27,6 +27,7 @@
 PER_STEP = 4
 STEPS = TILES // 2 // PER_STEP
 ES = PE * PER_STEP
+NETWORK = 8
 TS = 2 * PER_STEP
 
 SIDE = 11.0
@@ -57,6 +58,7 @@
 GROUPS = groups_of()
 NG = len(GROUPS)
 BLOCKS = NG + 1
+PLACE = {b: k for k, b in enumerate(OTHERS)}
 GROUP = {b: g for g, some in enumerate(GROUPS) for b in some}
 AT = {b: k * COUNT[b] for some in GROUPS for k, b in enumerate(some)}
 
@@ -156,6 +158,8 @@
     wht_ref,
     wrt_ref,
     wb3_ref,
+    placel_ref,
+    placer_ref,
     row_send,
     row_recv,
     xyz_send,
@@ -204,7 +208,7 @@
         order = sorted(some, key=lambda b: AT[26 - b])
         named = jnp.concatenate([lists_ref[b][:, 0 : COUNT[b]] for b in order], axis=1)
         chosen = hot(iota((ATOMS, 128), 0) == named)
-        chosen_ref[g] = chosen
+        chosen_ref[:, 128 * g : 128 * g + 128] = chosen
         out_rows[128 * g : 128 * g + 128, :] = dot(chosen, projected, 0, 0).astype(BF16)
         for d in range(3):
             shift = jnp.zeros((1, 128), F32)
@@ -217,32 +221,28 @@
 
     pl.semaphore_wait(barrier, 26)
 
-    row_copies, xyz_copies = [], []
+    for b in OTHERS:
+        pltpu.make_async_remote_copy(
+            src_ref=out_xyz.at[GROUP[b]],
+            dst_ref=in_xyz.at[PLACE[26 - b]],
+            send_sem=xyz_send,
+            recv_sem=xyz_recv,
+            device_id=device(b),
+            device_id_type=MESH,
+        ).start()
     for b in OTHERS:
         n, g, spot = COUNT[b], GROUP[b], AT[26 - b]
-        row_copies.append(
-            pltpu.make_async_remote_copy(
-                src_ref=out_rows.at[pl.ds(128 * g + spot, n), :],
-                dst_ref=table_b.at[pl.ds(128 * (g + 1) + spot, n), :],
-                send_sem=row_send.at[b],
-                recv_sem=row_recv.at[26 - b],
-                device_id=device(b),
-                device_id_type=MESH,
-            )
-        )
-        xyz_copies.append(
-            pltpu.make_async_remote_copy(
-                src_ref=out_xyz.at[g],
-                dst_ref=in_xyz.at[26 - b],
-                send_sem=xyz_send.at[b],
-                recv_sem=xyz_recv.at[26 - b],
-                device_id=device(b),
-                device_id_type=MESH,
-            )
-        )
-    for one, two in zip(row_copies, xyz_copies):
-        two.start()
-        one.start()
+        pltpu.make_async_remote_copy(
+            src_ref=out_rows.at[pl.ds(128 * g + spot, n), :],
+            dst_ref=table_b.at[pl.ds(128 * (g + 1) + spot, n), :],
+            send_sem=row_send,
+            recv_sem=row_recv,
+            device_id=device(b),
+            device_id_type=MESH,
+        ).start()
+
+    def wait_bytes(ref, sem):
+        pltpu.make_async_copy(ref, ref, sem).wait()
 
     for name in staged:
         if name not in early:
@@ -268,14 +268,17 @@
     target_ref[...] = receiver
 
     def place_lanes():
-        reach = hot(iota((TILES, JR), 1) // RT == iota((TILES, JR), 0))
-        expanded = dot(base_rows, reach, 1, 0).astype(I32) + iota((128, JR), 1) % RT
+        reach = hot((iota((TILES, JR), 1) >> 3) == iota((TILES, JR), 0))
+        expanded = dot(base_rows, reach, 1, 0).astype(I32) + (iota((128, JR), 1) & (RT - 1))
         return hot(expanded == iota((128, JR), 0))
 
     def place_rows():
-        reach = hot(iota((JR, TILES), 0) // RT == iota((JR, TILES), 1))
-        expanded = dot(reach, base_rows, 1, 1).astype(I32) + iota((JR, 128), 0) % RT
+        reach = hot((iota((JR, TILES), 0) >> 3) == iota((JR, TILES), 1))
+        expanded = dot(reach, base_rows, 1, 1).astype(I32) + (iota((JR, 128), 0) & (RT - 1))
         return hot(expanded == iota((JR, 128), 1))
+
+    placel_ref[...] = place_lanes()
+    placer_ref[...] = place_rows()
 
     block_lane = iota((1, 128), 1)
     moved_by = jnp.zeros((1, 128), I32)
@@ -289,14 +292,14 @@
         low_ref[at, :] = jnp.bitwise_and(entry, 127)
         high_ref[at, :] = jnp.right_shift(entry, 7)
 
-    for two in xyz_copies:
-        two.wait()
+    wait_bytes(in_xyz, xyz_recv)
+    wait_bytes(in_xyz, xyz_send)
     for d in range(3):
         table_c[0, d : d + 1, :] = own[d : d + 1, :]
     for g, some in enumerate(GROUPS):
-        value = in_xyz[some[0], 0:3, :]
+        value = in_xyz[PLACE[some[0]], 0:3, :]
         for b in some[1:]:
-            value = jnp.where(lane >= AT[b], in_xyz[b, 0:3, :], value)
+            value = jnp.where(lane >= AT[b], in_xyz[PLACE[b], 0:3, :], value)
         table_c[g + 1, 0:3, :] = value
 
     for g in range(TILES // 8):
@@ -326,16 +329,10 @@
         for m, value in enumerate(values):
             harm_ref[m, at, :] = value
 
-    for one in row_copies:
-        one.wait()
-    for k in range(BLOCKS):
-        block = table_b[128 * k : 128 * k + 128, :]
-        table_t[:, 128 * k : 128 * k + 128] = dot(eye, block, 1, 1).astype(BF16)
-
     decay = (iota((NB, PE), 0).astype(F32) + 1.0) * 0.5
     slot_ids = iota((RP, PE), 0)
     half_shift = jnp.where(iota((1, PE), 1) < EDGE, 0, RT)
-    row_ids = iota((128, PE), 0)
+    row_ids = iota((128, PE), 0).astype(F32).astype(BF16)
     inner = range(PER_STEP)
 
     def tiles_of(ref, first, count):
@@ -354,13 +351,13 @@
     def gather(pair):
         low = tiles_of(low_ref, 2 * pair, 2)
         high = tiles_of(high_ref, 2 * pair, 2)
-        at_low = hot(row_ids == low)
+        at_low = jnp.where(row_ids == low.astype(F32).astype(BF16), jnp.ones((), BF16), jnp.zeros((), BF16))
         at_ref[pair] = at_low
         entries = jnp.concatenate([at_low * hot(high == k) for k in range(BLOCKS)], axis=0)
         rows_ref[pair] = dot(table_t[...], entries, 1, 0).astype(BF16)
 
-    def network(step):
-        pairs = [step * PER_STEP + q for q in inner]
+    def network(step, carry):
+        pairs = [step * NETWORK + q for q in range(NETWORK)]
         basis4 = []
         for pair in pairs:
             s, reach, fall = radial_parts(pair)
@@ -369,8 +366,6 @@
             lo = basis - hi
             basis4.append(jnp.concatenate([hi, lo, hi, lo], axis=0).astype(BF16))
         pre1 = [dot(wbt_ref[...], value, 1, 0) for value in basis4]
-        for pair in pairs[: PER_STEP // 2]:
-            gather(pair)
         act1 = []
         for pair, pre in zip(pairs, pre1):
             sig = sigmoid(pre)
@@ -378,13 +373,20 @@
             d1_ref[pair] = sig + act * (1.0 - sig)
             act1.append(act.astype(BF16))
         pre2 = [dot(wht_ref[...], value, 1, 0) for value in act1]
-        for pair in pairs[PER_STEP // 2 :]:
-            gather(pair)
         for pair, pre in zip(pairs, pre2):
             sig = sigmoid(pre)
             act = pre * sig
             d2_ref[pair] = sig + act * (1.0 - sig)
             h2_ref[pair] = act.astype(BF16)
+        return carry
+
+    lax.fori_loop(0, TILES // 2 // NETWORK, network, 0)
+
+    wait_bytes(table_b.at[pl.ds(ATOMS, NG * 128), :], row_recv)
+    wait_bytes(out_rows, row_send)
+    for k in range(BLOCKS):
+        block = table_b[128 * k : 128 * k + 128, :]
+        table_t[:, 128 * k : 128 * k + 128] = dot(eye, block, 1, 1).astype(BF16)
 
     def gathered(step):
         for q in inner:
@@ -410,13 +412,14 @@
 
     def forward(step, carry):
         gathered(lax.rem(step + (STEPS - 1), STEPS))
-        network(step)
+        for q in inner:
+            gather(step * PER_STEP + q)
         return carry
 
     lax.fori_loop(0, STEPS, forward, 0)
     gathered(STEPS - 1)
 
-    sums = dot(place_lanes(), p_ref[...], 1, 0)
+    sums = dot(placel_ref[...], p_ref[...], 1, 0)
     halves = [0.5 * sums[:, m * C : m * C + C] for m in range(9)]
     inv = [halves[0]]
     for first, last in SPANS[1:]:
@@ -443,7 +446,7 @@
         part = dinv[:, DEGREE[m] * C : DEGREE[m] * C + C]
         grads.append(0.5 * part if m == 0 else halves[m] * part)
     grads = jnp.concatenate(grads, axis=1).astype(BF16)
-    s_ref[...] = dot(place_rows(), grads, 1, 0).astype(BF16)
+    s_ref[...] = dot(placer_ref[...], grads, 1, 0).astype(BF16)
 
     acc_ref[...] = jnp.zeros_like(acc_ref)
     racc_ref[...] = jnp.zeros_like(racc_ref)
@@ -529,32 +532,30 @@
         mine = racc_ref[2 * d : 2 * d + 1, :] + racc_ref[2 * d + 1 : 2 * d + 2, :]
         force_ref[d] = mine - grid[0:1, :]
 
-    grad_copies = []
     for b in OTHERS:
-        copy = pltpu.make_async_remote_copy(
+        pltpu.make_async_remote_copy(
             src_ref=out_grad.at[GROUP[b]],
-            dst_ref=in_grad.at[26 - b],
-            send_sem=grad_send.at[b],
-            recv_sem=grad_recv.at[26 - b],
+            dst_ref=in_grad.at[PLACE[26 - b]],
+            send_sem=grad_send,
+            recv_sem=grad_recv,
             device_id=device(b),
             device_id_type=MESH,
-        )
-        copy.start()
-        grad_copies.append(copy)
-    for copy in grad_copies:
-        copy.wait()
-
-    total = jnp.zeros((8, ATOMS), F32)
-    row8 = iota((8, 128), 0)
-    for g, some in enumerate(GROUPS):
+        ).start()
+    wait_bytes(in_grad, grad_recv)
+    wait_bytes(in_grad, grad_send)
+
+    stacks = []
+    for some in GROUPS:
         order = sorted(some, key=lambda b: AT[26 - b])
-        came = in_grad[order[0]]
+        came = in_grad[PLACE[order[0]], 0:3, :]
         for b in order[1:]:
-            came = jnp.where(lane >= AT[26 - b], in_grad[b], came)
-        hi, lo = split(jnp.where(row8 < 3, came, 0.0))
-        total = total + dot(hi, chosen_ref[g], 1, 1) + dot(lo, chosen_ref[g], 1, 1)
+            came = jnp.where(lane >= AT[26 - b], in_grad[PLACE[b], 0:3, :], came)
+        hi = came.astype(BF16).astype(F32)
+        stacks.append(jnp.concatenate([hi, came - hi], axis=0))
+    stacks = jnp.concatenate(stacks, axis=1).astype(BF16)
+    total = dot(stacks, chosen_ref[...], 1, 1)
     for d in range(3):
-        force_ref[d] = force_ref[d] - total[d : d + 1, :]
+        force_ref[d] = force_ref[d] - (total[d : d + 1, :] + total[d + 3 : d + 4, :])
 
 
 def solution(mesh):
@@ -579,7 +580,7 @@
         tile_bases,
         tile_live,
     ):
-        dma = pltpu.SemaphoreType.DMA((27,))
+        dma = pltpu.SemaphoreType.DMA
         force, energy = pl.pallas_call(
             functools.partial(kernel, sizes),
             out_shape=(
@@ -605,12 +606,12 @@
                 pltpu.SMEM((1, 1), I32),
                 pltpu.SemaphoreType.DMA((14,)),
                 pltpu.VMEM((NG * 128, C), BF16),
-                pltpu.VMEM((NG, 8, 128), F32),
+                pltpu.VMEM((NG, 4, 128), F32),
                 pltpu.VMEM((BLOCKS * 128, C), BF16),
-                pltpu.VMEM((27, 8, 128), F32),
+                pltpu.VMEM((26, 4, 128), F32),
                 pltpu.VMEM((C, BLOCKS * 128), BF16),
                 pltpu.VMEM((BLOCKS, 8, 128), F32),
-                pltpu.VMEM((NG, ATOMS, 128), BF16),
+                pltpu.VMEM((ATOMS, NG * 128), BF16),
                 pltpu.VMEM((pairs, 128, PE), BF16),
                 pltpu.VMEM((pairs, RH, PE), BF16),
                 pltpu.VMEM((pairs, C, PE), BF16),
@@ -633,12 +634,14 @@
                 pltpu.VMEM((6, TS, EDGE), F32),
                 pltpu.VMEM((48, 128), F32),
                 pltpu.VMEM((8, 128), F32),
-                pltpu.VMEM((NG, 8, 128), F32),
-                pltpu.VMEM((27, 8, 128), F32),
+                pltpu.VMEM((NG, 4, 128), F32),
+                pltpu.VMEM((26, 4, 128), F32),
                 pltpu.VMEM((RH, 4 * NB), BF16),
                 pltpu.VMEM((RH, RH), BF16),
                 pltpu.VMEM((3 * C, RH), BF16),
                 pltpu.VMEM((NB, 3 * RH), BF16),
+                pltpu.VMEM((ATOMS, JR), BF16),
+                pltpu.VMEM((JR, ATOMS), BF16),
                 dma,
                 dma,
                 dma,

time: 57.7 us -> 53.8 us (0.932)
  Pallas kernels: 54.3 us -> 50.5 us
    pallas_call x1, Pallas kernels: 54.3 us -> 50.5 us  [step(): pl.pallas_call(functools.partial(kernel, sizes), out_shape=(jax.ShapeDtyp...]
where the time goes in v3:
time: 53.8 us; the launch traced here: 53.6 us
  Pallas kernels  50.5 us (94%)
  local copies, waits for them, and re-layouts  1.8 us (3%)
  between operations  1.3 us (2%)
    pallas_call x1, Pallas kernels, step(): pl.pallas_call(functools.partial(kernel, sizes), out_shape=(jax.ShapeDtyp...  50.5 us
    unnamed x6, local copies, waits for them, and re-layouts  1.8 us

profile of v3, /device:TPU:8, one launch (start us, length us, event | category | flops | bytes accessed | tf_op | source)
XLA Modules:
  0.0 53.6 jit_solution(4705921985720051721)
XLA Ops:
  1.3 50.5 %shard_map.149 = (f32[3,1,128]{2,1,0:T(1,128)}, f32[1,128]{1,0:T(1,128)}) custom-call(bf16[128,128]{1,0:T(8,128)(2,1)} %bitcast.13, f32[3,1,128]{2,1,0:T(1,128)} %bitcast.18, bf16[128,128]{1,0:T(8,128)(2,1)} %wup_hbm.1, f32[8,64]{1,0:T(8,128)} %wbasis_hbm.1, bf16[64,64]{1,0:T(8,128)(2,1)} %whid_hbm.1, bf16[64,384]{1,0:T(8,128)(2,1)} %wrad_hbm.1, ...), custom_call_target="tpu_custom_call" | custom-call | tf_op jit(solution)/shard_map/pallas_call | solution.py:584
  51.8 0.0 copy-start
  51.8 0.7 %copy-done = f32[3,1,128]{2,1,0:T(1,128)S(1)} copy-done((f32[3,1,128]{2,1,0:T(1,128)S(1)}, f32[3,1,128]{2,1,0:T(1,128)}, u32[]{:S(2)}) %copy-start) | copy-done | bytes 1560
  52.5 0.0 copy-start.1
  52.5 0.6 %copy.20 = f32[1,1,1,3,128]{4,2,3,1,0:T(1,128)} copy(f32[1,1,1,3,128]{4,2,3,1,0:T(1,128)S(1)} %bitcast.19) | data formatting | bytes 3072
  53.0 0.1 copy-done.1
  53.1 0.5 copy.21
Async XLA Ops:
  51.8 0.7 %copy-start = (f32[3,1,128]{2,1,0:T(1,128)S(1)}, f32[3,1,128]{2,1,0:T(1,128)}, u32[]{:S(2)}) copy-start(f32[3,1,128]{2,1,0:T(1,128)} %get-tuple-element.4) | copy-start | bytes 4612
  52.5 0.6 %copy-start.1 = (f32[1,128]{1,0:T(1,128)S(1)}, f32[1,128]{1,0:T(1,128)}, u32[]{:S(2)}) copy-start(f32[1,128]{1,0:T(1,128)} %get-tuple-element.5) | copy-start | bytes 1540

commit v4 on v3

--- a/solution.py
+++ b/solution.py
@@ -107,7 +107,6 @@
     base_hbm,
     live_hbm,
     force_ref,
-    energy_ref,
     feat_ref,
     pos_ref,
     wup_ref,
@@ -172,16 +171,12 @@
     def device(b):
         return tuple(lax.rem(c + (d + n), n) for c, d, n in zip(here, DIRS[b], sizes))
 
-    barrier = pltpu.get_barrier_semaphore()
-    for b in OTHERS:
-        pl.semaphore_signal(barrier, inc=1, device_id=device(b), device_id_type=MESH)
-
     staged = {}
     moves = (
+        ("lists", lists_hbm, lists_ref),
+        ("pos", pos_hbm, pos_ref),
         ("feat", feat_hbm, feat_ref),
         ("wup", wup_hbm, wup_ref),
-        ("lists", lists_hbm, lists_ref),
-        ("pos", pos_hbm, pos_ref),
         ("base", base_hbm, base_ref),
         ("live", live_hbm, live_ref),
         ("slot", slot_hbm, slot_ref),
@@ -193,23 +188,26 @@
         ("wread", wread_hbm, wread_ref),
         ("wout", wout_hbm, wout_ref),
     )
+    early = ("lists", "pos", "feat", "wup")
     for k, (name, source, target) in enumerate(moves):
         staged[name] = pltpu.make_async_copy(source, target, stage_sem.at[k])
-        staged[name].start()
-    early = ("feat", "wup", "lists", "pos")
-    for name in early:
-        staged[name].wait()
-
-    projected = dot(feat_ref[...], wup_ref[...], 1, 0).astype(BF16)
-    table_b[0:ATOMS, :] = projected
+        if name in early:
+            staged[name].start()
+    barrier = pltpu.get_barrier_semaphore()
+    for b in OTHERS:
+        pl.semaphore_signal(barrier, inc=1, device_id=device(b), device_id_type=MESH)
+    for name in staged:
+        if name not in early:
+            staged[name].start()
+
+    staged["lists"].wait()
+    staged["pos"].wait()
     own = jnp.concatenate([pos_ref[d] for d in range(3)], axis=0)
     lane = iota((1, 128), 1)
     for g, some in enumerate(GROUPS):
         order = sorted(some, key=lambda b: AT[26 - b])
         named = jnp.concatenate([lists_ref[b][:, 0 : COUNT[b]] for b in order], axis=1)
-        chosen = hot(iota((ATOMS, 128), 0) == named)
-        chosen_ref[:, 128 * g : 128 * g + 128] = chosen
-        out_rows[128 * g : 128 * g + 128, :] = dot(chosen, projected, 0, 0).astype(BF16)
+        chosen_ref[:, 128 * g : 128 * g + 128] = hot(iota((ATOMS, 128), 0) == named)
         for d in range(3):
             shift = jnp.zeros((1, 128), F32)
             for b in some:
@@ -230,6 +228,13 @@
             device_id=device(b),
             device_id_type=MESH,
         ).start()
+    staged["feat"].wait()
+    staged["wup"].wait()
+    projected = dot(feat_ref[...], wup_ref[...], 1, 0).astype(BF16)
+    table_b[0:ATOMS, :] = projected
+    for g in range(NG):
+        at = slice(128 * g, 128 * g + 128)
+        out_rows[at, :] = dot(chosen_ref[:, at], projected, 0, 0).astype(BF16)
     for b in OTHERS:
         n, g, spot = COUNT[b], GROUP[b], AT[26 - b]
         pltpu.make_async_remote_copy(
@@ -258,7 +263,7 @@
     for degree in range(3):
         part = wrad_ref[:, degree * C : degree * C + C]
         wrt_ref[degree * C : degree * C + C, :] = dot(eye, part, 1, 1).astype(BF16)
-    wb3_ref[...] = jnp.concatenate([hi, hi, lo], axis=1).astype(BF16)
+    wb3_ref[...] = jnp.concatenate([hi, lo], axis=0).astype(BF16)
 
     base_rows = jnp.broadcast_to(base_ref[...].astype(F32), (128, TILES)).astype(BF16)
     eye_tiles = hot(iota((TILES, TILES), 0) == iota((TILES, TILES), 1))
@@ -437,7 +442,7 @@
     outw = jnp.zeros((RO, ATOMS), F32)
     for r in range(RO):
         outw = jnp.where(row == r, wout_ref[r], outw)
-    energy_ref[...] = jnp.sum(outw * act, axis=0, keepdims=True)
+    force_ref[3] = jnp.sum(outw * act, axis=0, keepdims=True)
     dpre = outw * (sig + act * (1.0 - sig))
     dupd = dot(dpre, wread_ref[...], 0, 0, high)
     dinv = dot(dupd.astype(BF16), wmix_ref[...], 1, 1).astype(BF16).astype(F32)
@@ -479,9 +484,9 @@
         dact1 = [dot(whid_ref[...], value, 1, 0) for value in dpre2]
         stacks = []
         for value, pair in zip(dact1, pairs):
-            hi, lo = split(value * d1_ref[pair])
-            stacks.append(jnp.concatenate([hi, lo, hi], axis=0))
+            stacks.append((value * d1_ref[pair]).astype(BF16))
         dbasis = [dot(wb3_ref[...], value, 1, 0) for value in stacks]
+        dbasis = [value[0:NB, :] + value[NB : 2 * NB, :] for value in dbasis]
         for value, pair in zip(dbasis, pairs):
             s, reach, fall = radial_parts(pair)
             slope = fall * (-decay * (reach * reach) - (4.0 * s) * reach)
@@ -581,14 +586,11 @@
         tile_live,
     ):
         dma = pltpu.SemaphoreType.DMA
-        force, energy = pl.pallas_call(
+        both = pl.pallas_call(
             functools.partial(kernel, sizes),
-            out_shape=(
-                jax.ShapeDtypeStruct((3, 1, ATOMS), F32),
-                jax.ShapeDtypeStruct((1, ATOMS), F32),
-            ),
+            out_shape=jax.ShapeDtypeStruct((4, 1, ATOMS), F32),
             in_specs=[hbm] * 14,
-            out_specs=(vmem, vmem),
+            out_specs=vmem,
             scratch_shapes=[
                 pltpu.VMEM((ATOMS, C), BF16),
                 pltpu.VMEM((3, 1, ATOMS), F32),
@@ -639,7 +641,7 @@
                 pltpu.VMEM((RH, 4 * NB), BF16),
                 pltpu.VMEM((RH, RH), BF16),
                 pltpu.VMEM((3 * C, RH), BF16),
-                pltpu.VMEM((NB, 3 * RH), BF16),
+                pltpu.VMEM((2 * NB, RH), BF16),
                 pltpu.VMEM((ATOMS, JR), BF16),
                 pltpu.VMEM((JR, ATOMS), BF16),
                 dma,
@@ -670,7 +672,7 @@
             tile_bases.reshape(1, TILES),
             tile_live.reshape(1, 1),
         )
-        return force.reshape(1, 1, 1, 3, ATOMS), energy.reshape(1, 1, 1, ATOMS)
+        return both[0:3].reshape(1, 1, 1, 3, ATOMS), both[3].reshape(1, 1, 1, ATOMS)
 
     cube = ("gx", "gy", "gz")
     return jax.shard_map(

time: 53.8 us -> 54.3 us (level)
  local copies, waits for them, and re-layouts: 1.8 us -> 2.44 us
    another operation x0 -> x1, local copies, waits for them, and re-layouts: none -> 1.19 us  [step(): both[3].reshape(1, 1, 1, ATOMS)]
    unnamed x6 -> x1, local copies, waits for them, and re-layouts: 1.8 us -> 1.24 us
where the time goes in v4:
time: 54.3 us; the launch traced here: 54.1 us
  Pallas kernels  50.3 us (93%)
  local copies, waits for them, and re-layouts  2.44 us (4%)
  between operations  1.29 us (2%)
    pallas_call x1, Pallas kernels, step(): pl.pallas_call(functools.partial(kernel, sizes), out_shape=jax.ShapeDtype...  50.3 us
    unnamed x1, local copies, waits for them, and re-layouts  1.24 us
    another operation x1, local copies, waits for them, and re-layouts, step(): both[3].reshape(1, 1, 1, ATOMS)  1.19 us

profile of v4, /device:TPU:8, one launch (start us, length us, event | category | flops | bytes accessed | tf_op | source)
XLA Modules:
  0.0 54.1 jit_solution(16555350508777622823)
XLA Ops:
  1.3 50.3 %shard_map.149 = f32[4,1,128]{2,1,0:T(1,128)} custom-call(bf16[128,128]{1,0:T(8,128)(2,1)} %bitcast.15, f32[3,1,128]{2,1,0:T(1,128)} %bitcast.20, bf16[128,128]{1,0:T(8,128)(2,1)} %wup_hbm.1, f32[8,64]{1,0:T(8,128)} %wbasis_hbm.1, bf16[64,64]{1,0:T(8,128)(2,1)} %whid_hbm.1, bf16[64,384]{1,0:T(8,128)(2,1)} %wrad_hbm.1, bf16[384,128]{1,0:T(8,128)(2,1)} %wmix_hbm.1, ...), custom_call_target="tpu_custom_call" | custom-call | tf_op jit(solution)/shard_map/pallas_call | solution.py:589
  51.6 1.2 %slice_bitcast_fusion.1 = f32[1,1,1,128]{3,2,1,0:T(1,128)} fusion(f32[4,1,128]{2,1,0:T(1,128)} %shard_map.149), kind=kLoop, calls=%fused_computation.1 | loop fusion | bytes 1024 | tf_op jit(solution)/shard_map/reshape;squeeze | solution.py:675
  52.8 1.2 %slice_bitcast_fusion = f32[1,1,1,3,128]{4,2,3,1,0:T(1,128)} fusion(f32[4,1,128]{2,1,0:T(1,128)} %shard_map.149), kind=kLoop, calls=%fused_computation | loop fusion | bytes 3072

commit v5 on v4

--- a/solution.py
+++ b/solution.py
@@ -26,9 +26,11 @@
 RP = 2 * RT
 PER_STEP = 4
 STEPS = TILES // 2 // PER_STEP
-ES = PE * PER_STEP
+BACK = 8
+BSTEPS = TILES // 2 // BACK
+ES = PE * BACK
 NETWORK = 8
-TS = 2 * PER_STEP
+TS = 2 * BACK
 
 SIDE = 11.0
 INV_CUT = 0.2
@@ -107,6 +109,7 @@
     base_hbm,
     live_hbm,
     force_ref,
+    energy_ref,
     feat_ref,
     pos_ref,
     wup_ref,
@@ -133,7 +136,6 @@
     h2_ref,
     rows_ref,
     g_ref,
-    dr_ref,
     a_ref,
     d1_ref,
     d2_ref,
@@ -359,7 +361,9 @@
         at_low = jnp.where(row_ids == low.astype(F32).astype(BF16), jnp.ones((), BF16), jnp.zeros((), BF16))
         at_ref[pair] = at_low
         entries = jnp.concatenate([at_low * hot(high == k) for k in range(BLOCKS)], axis=0)
-        rows_ref[pair] = dot(table_t[...], entries, 1, 0).astype(BF16)
+        rows = dot(table_t[...], entries, 1, 0).astype(BF16)
+        rows_ref[pair] = rows
+        return rows
 
     def network(step, carry):
         pairs = [step * NETWORK + q for q in range(NETWORK)]
@@ -393,7 +397,7 @@
         block = table_b[128 * k : 128 * k + 128, :]
         table_t[:, 128 * k : 128 * k + 128] = dot(eye, block, 1, 1).astype(BF16)
 
-    def gathered(step):
+    def gathered(step, values, radials):
         for q in inner:
             pair = step * PER_STEP + q
             onehot = onehot_of(2 * pair)
@@ -402,9 +406,9 @@
                 weights.append(onehot * tiles_of(harm_ref.at[m], 2 * pair, 2))
             weights = jnp.concatenate(weights, axis=0).astype(BF16)
             a_ref[pair] = weights
-            rows = rows_ref[pair]
+            rows = values[q]
             place = pl.ds(pair * RP, RP)
-            radial = dot(wrt_ref[...], h2_ref[pair], 1, 0).astype(BF16)
+            radial = radials[q]
             for degree, (first, last) in enumerate(SPANS):
                 across = slice(degree * C, degree * C + C)
                 g = radial[across, :] * rows
@@ -416,13 +420,11 @@
                     ]
 
     def forward(step, carry):
-        gathered(lax.rem(step + (STEPS - 1), STEPS))
-        for q in inner:
-            gather(step * PER_STEP + q)
+        radials = [dot(wrt_ref[...], h2_ref[step * PER_STEP + q], 1, 0).astype(BF16) for q in inner]
+        gathered(step, [gather(step * PER_STEP + q) for q in inner], radials)
         return carry
 
     lax.fori_loop(0, STEPS, forward, 0)
-    gathered(STEPS - 1)
 
     sums = dot(placel_ref[...], p_ref[...], 1, 0)
     halves = [0.5 * sums[:, m * C : m * C + C] for m in range(9)]
@@ -442,7 +444,7 @@
     outw = jnp.zeros((RO, ATOMS), F32)
     for r in range(RO):
         outw = jnp.where(row == r, wout_ref[r], outw)
-    force_ref[3] = jnp.sum(outw * act, axis=0, keepdims=True)
+    energy_ref[...] = jnp.sum(outw * act, axis=0, keepdims=True)
     dpre = outw * (sig + act * (1.0 - sig))
     dupd = dot(dpre, wread_ref[...], 0, 0, high)
     dinv = dot(dupd.astype(BF16), wmix_ref[...], 1, 1).astype(BF16).astype(F32)
@@ -456,36 +458,45 @@
     acc_ref[...] = jnp.zeros_like(acc_ref)
     racc_ref[...] = jnp.zeros_like(racc_ref)
 
-    def to_edges(step):
-        for q in inner:
-            pair = step * PER_STEP + q
-            onehot = onehot_of(2 * pair)
-            place = pl.ds(pair * RP, RP)
-            rows = rows_ref[pair]
-            for degree, (first, last) in enumerate(SPANS):
-                cot = jnp.concatenate(
-                    [s_ref[place, m * C : m * C + C] for m in range(first, last)], axis=0
-                )
+    def cotangents(pair, first, last):
+        place = pl.ds(pair * RP, RP)
+        return jnp.concatenate(
+            [s_ref[place, m * C : m * C + C] for m in range(first, last)], axis=0
+        )
+
+    def row_gradients(pair):
+        rows = rows_ref[pair]
+        parts = []
+        for first, last in SPANS:
+            cot = cotangents(pair, first, last)
+            dg = dot(cot, a_ref[pair, first * RP : last * RP, :], 0, 0)
+            parts.append(dg.astype(BF16) * rows)
+        return jnp.concatenate(parts, axis=0)
+
+    def harmonic_gradients(pair):
+        onehot = onehot_of(2 * pair)
+        for degree, (first, last) in enumerate(SPANS):
+            if degree:
                 across = slice(degree * C, degree * C + C)
-                dg = dot(cot, a_ref[pair, first * RP : last * RP, :], 0, 0)
-                dr_ref[pair, across, :] = dg.astype(BF16) * rows
-                if degree:
-                    back = dot(cot, g_ref[pair, across, :], 1, 0)
-                    for m in range(first, last):
-                        one = back[(m - first) * RP : (m - first) * RP + RP, :]
-                        dh = jnp.sum(one * onehot, axis=0, keepdims=True)
-                        dharm_ref[m, pl.ds(2 * pair, 1), :] = dh[:, 0:EDGE]
-                        dharm_ref[m, pl.ds(2 * pair + 1, 1), :] = dh[:, EDGE:PE]
-
-    def to_radius(step):
-        pairs = [step * PER_STEP + q for q in inner]
-        dact2 = [dot(wrad_ref[...], dr_ref[pair], 1, 0) for pair in pairs]
+                back = dot(cotangents(pair, first, last), g_ref[pair, across, :], 1, 0)
+                for m in range(first, last):
+                    one = back[(m - first) * RP : (m - first) * RP + RP, :]
+                    dh = jnp.sum(one * onehot, axis=0, keepdims=True)
+                    dharm_ref[m, pl.ds(2 * pair, 1), :] = dh[:, 0:EDGE]
+                    dharm_ref[m, pl.ds(2 * pair + 1, 1), :] = dh[:, EDGE:PE]
+
+    def gradients(step):
+        pairs = [step * BACK + q for q in range(BACK)]
+        dradial = [row_gradients(pair) for pair in pairs]
+        dact2 = [dot(wrad_ref[...], value, 1, 0) for value in dradial]
         dpre2 = [(value * d2_ref[pair]).astype(BF16) for value, pair in zip(dact2, pairs)]
+        for pair in pairs[: BACK // 2]:
+            harmonic_gradients(pair)
         dact1 = [dot(whid_ref[...], value, 1, 0) for value in dpre2]
-        stacks = []
-        for value, pair in zip(dact1, pairs):
-            stacks.append((value * d1_ref[pair]).astype(BF16))
-        dbasis = [dot(wb3_ref[...], value, 1, 0) for value in stacks]
+        for pair in pairs[BACK // 2 :]:
+            harmonic_gradients(pair)
+        dpre1 = [(value * d1_ref[pair]).astype(BF16) for value, pair in zip(dact1, pairs)]
+        dbasis = [dot(wb3_ref[...], value, 1, 0) for value in dpre1]
         dbasis = [value[0:NB, :] + value[NB : 2 * NB, :] for value in dbasis]
         for value, pair in zip(dbasis, pairs):
             s, reach, fall = radial_parts(pair)
@@ -508,8 +519,8 @@
             gsep_ref[2 * d] = hi
             gsep_ref[2 * d + 1] = g - hi
         at_high = iota((8, ES), 0) == tiles_of(high_ref, step * TS, TS)
-        at_target = hot(iota((128, ES), 0) == tiles_of(target_ref, step * TS, TS))
-        at_low = jnp.concatenate([at_ref[step * PER_STEP + q] for q in inner], axis=1)
+        at_target = jnp.where(iota((128, ES), 0).astype(F32).astype(BF16) == tiles_of(target_ref, step * TS, TS).astype(F32).astype(BF16), jnp.ones((), BF16), jnp.zeros((), BF16))
+        at_low = jnp.concatenate([at_ref[step * BACK + q] for q in range(BACK)], axis=1)
         row8 = iota((8, ES), 0)
         left, stack = [], jnp.zeros((8, ES), F32)
         for k in range(6):
@@ -520,15 +531,12 @@
         racc_ref[...] += dot(stack.astype(BF16), at_target, 1, 1)
 
     def backward(step, carry):
-        scatter(lax.rem(step + (STEPS - 2), STEPS), step >= 2)
-        to_radius(lax.rem(step + (STEPS - 1), STEPS))
-        to_edges(step)
+        scatter(lax.rem(step + (BSTEPS - 1), BSTEPS), step >= 1)
+        gradients(step)
         return carry
 
-    lax.fori_loop(0, STEPS, backward, 0)
-    scatter(STEPS - 2, True)
-    to_radius(STEPS - 1)
-    scatter(STEPS - 1, True)
+    lax.fori_loop(0, BSTEPS, backward, 0)
+    scatter(BSTEPS - 1, True)
 
     for d in range(3):
         grid = acc_ref[16 * d : 16 * d + 8, :] + acc_ref[16 * d + 8 : 16 * d + 16, :]
@@ -586,11 +594,14 @@
         tile_live,
     ):
         dma = pltpu.SemaphoreType.DMA
-        both = pl.pallas_call(
+        force, energy = pl.pallas_call(
             functools.partial(kernel, sizes),
-            out_shape=jax.ShapeDtypeStruct((4, 1, ATOMS), F32),
+            out_shape=(
+                jax.ShapeDtypeStruct((3, 1, ATOMS), F32),
+                jax.ShapeDtypeStruct((1, ATOMS), F32),
+            ),
             in_specs=[hbm] * 14,
-            out_specs=vmem,
+            out_specs=(vmem, vmem),
             scratch_shapes=[
                 pltpu.VMEM((ATOMS, C), BF16),
                 pltpu.VMEM((3, 1, ATOMS), F32),
@@ -617,7 +628,6 @@
                 pltpu.VMEM((pairs, 128, PE), BF16),
                 pltpu.VMEM((pairs, RH, PE), BF16),
                 pltpu.VMEM((pairs, C, PE), BF16),
-                pltpu.VMEM((pairs, 3 * C, PE), BF16),
                 pltpu.VMEM((pairs, 3 * C, PE), BF16),
                 pltpu.VMEM((pairs, 9 * RP, PE), BF16),
                 pltpu.VMEM((pairs, RH, PE), F32),
@@ -672,7 +682,7 @@
             tile_bases.reshape(1, TILES),
             tile_live.reshape(1, 1),
         )
-        return both[0:3].reshape(1, 1, 1, 3, ATOMS), both[3].reshape(1, 1, 1, ATOMS)
+        return force.reshape(1, 1, 1, 3, ATOMS), energy.reshape(1, 1, 1, ATOMS)
 
     cube = ("gx", "gy", "gz")
     return jax.shard_map(

time: 54.3 us -> 49.6 us (0.913)
  Pallas kernels: 50.3 us -> 46.2 us
  local copies, waits for them, and re-layouts: 2.44 us -> 1.8 us
    pallas_call x1, Pallas kernels: 50.3 us -> 46.2 us  [step(): pl.pallas_call(functools.partial(kernel, sizes), out_shape=(jax.ShapeDtyp...]
    another operation x1 -> x0, local copies, waits for them, and re-layouts: 1.19 us -> none  [step(): both[3].reshape(1, 1, 1, ATOMS)]
    unnamed x1 -> x6, local copies, waits for them, and re-layouts: 1.24 us -> 1.8 us
where the time goes in v5:
time: 49.6 us; the launch traced here: 49.4 us
  Pallas kernels  46.2 us (93%)
  local copies, waits for them, and re-layouts  1.8 us (4%)
  between operations  1.3 us (3%)
    pallas_call x1, Pallas kernels, step(): pl.pallas_call(functools.partial(kernel, sizes), out_shape=(jax.ShapeDtyp...  46.2 us
    unnamed x6, local copies, waits for them, and re-layouts  1.8 us

profile of v5, /device:TPU:8, one launch (start us, length us, event | category | flops | bytes accessed | tf_op | source)
XLA Modules:
  0.0 49.4 jit_solution(11264860729836615173)
XLA Ops:
  1.3 46.2 %shard_map.149 = (f32[3,1,128]{2,1,0:T(1,128)}, f32[1,128]{1,0:T(1,128)}) custom-call(bf16[128,128]{1,0:T(8,128)(2,1)} %bitcast.13, f32[3,1,128]{2,1,0:T(1,128)} %bitcast.18, bf16[128,128]{1,0:T(8,128)(2,1)} %wup_hbm.1, f32[8,64]{1,0:T(8,128)} %wbasis_hbm.1, bf16[64,64]{1,0:T(8,128)(2,1)} %whid_hbm.1, bf16[64,384]{1,0:T(8,128)(2,1)} %wrad_hbm.1, ...), custom_call_target="tpu_custom_call" | custom-call | tf_op jit(solution)/shard_map/pallas_call | solution.py:597
  47.5 0.0 copy-start
  47.5 0.7 %copy-done = f32[3,1,128]{2,1,0:T(1,128)S(1)} copy-done((f32[3,1,128]{2,1,0:T(1,128)S(1)}, f32[3,1,128]{2,1,0:T(1,128)}, u32[]{:S(2)}) %copy-start) | copy-done | bytes 1560
  48.2 0.0 copy-start.1
  48.2 0.6 %copy.20 = f32[1,1,1,3,128]{4,2,3,1,0:T(1,128)} copy(f32[1,1,1,3,128]{4,2,3,1,0:T(1,128)S(1)} %bitcast.19) | data formatting | bytes 3072
  48.8 0.1 copy-done.1
  48.8 0.5 %copy.21 = f32[1,1,1,128]{3,2,1,0:T(1,128)} copy(f32[1,1,1,128]{3,2,1,0:T(1,128)S(1)} %bitcast.21) | data formatting | bytes 1024
Async XLA Ops:
  47.5 0.7 %copy-start = (f32[3,1,128]{2,1,0:T(1,128)S(1)}, f32[3,1,128]{2,1,0:T(1,128)}, u32[]{:S(2)}) copy-start(f32[3,1,128]{2,1,0:T(1,128)} %get-tuple-element.4) | copy-start | bytes 4612
  48.2 0.6 %copy-start.1 = (f32[1,128]{1,0:T(1,128)S(1)}, f32[1,128]{1,0:T(1,128)}, u32[]{:S(2)}) copy-start(f32[1,128]{1,0:T(1,128)} %get-tuple-element.5) | copy-start | bytes 1540
